TPU v7x, 32 devices: a whole 2x2x4 slice. The times are simulated.
32 devices in a mesh: lat: 4 (over z), lon: 8 (over y, x, core).
Axes of the slice: x: 2, y: 2, z: 4, core: 2. Of those that a mesh axis runs over, the one named last changes fastest.
Arguments:
- radiances: bfloat16 [32768, 8461], P(('lat', 'lon')), may hold values from -6 to 6
- project_weight: bfloat16 [8461, 256], replicated, may hold values from -0.0625 to 0.0625
- tile_ids: int32 [32768], P(('lat', 'lon')), may hold values from 0 to 31, as said below
- slot_offsets: int32 [32768], P(('lat', 'lon')), may hold values from 0 to 2559, as said below
- tile_counts: int32 [4, 8], P('lat', 'lon'), may hold values from 512 to 2560, as said below
- setconv_weights: bfloat16 [256, 256, 2560], P('lat', 'lon'), may hold values from 0.049804688 to 1
- conv1_weight: bfloat16 [3, 3, 256, 256], replicated, may hold values from -0.125 to 0.125
- conv2_weight: bfloat16 [3, 3, 256, 256], replicated, may hold values from -0.125 to 0.125
Outputs:
- encoded: bfloat16 [64, 64, 256], P('lat', 'lon')
Inputs may be any that keep to these rules, and one draw needn't show every extreme that they name: `tile_ids`: A device's observations bound for one tile stand next to each other; one device sends at most 112 observations to one tile, a number reached in every draw. `slot_offsets`: the observations bound for one tile hold the offsets 0 to its count minus 1, each once. `tile_counts`: each entry is the number of observations whose tile_ids name that tile; 2560 is reached in every draw.
All inputs are finite; a program needn't handle non-finite values.
Results may differ from a plain program's by a relative error of at most 0.009.
Values may be sent and summed in bfloat16 or wider, within the bound.
A program may use at most 512 MiB of HBM per device.

v0:
```python
import jax
import jax.numpy as jnp
from jax import lax
from jax.sharding import PartitionSpec as P


def shifted_2(value, axis, by):
    peers = lax.axis_size(axis)
    pairs = [(i, i + by) for i in range(peers) if 0 <= i + by < peers]
    return lax.ppermute(value, axis, pairs)


def passed_along(value, axis, steps):
    count = lax.axis_size(axis)
    pairs = [(source, (source + steps) % count) for source in range(count)]
    return lax.ppermute(value, axis, pairs)


def stride_conv(field, kernel):
    height, breadth, depth = field.shape
    half_rows, half_cols = (height // 2, breadth // 2)
    upper_rim = shifted_2(field[-1:], "lat", 1)
    west_column = jnp.concatenate([upper_rim[:, -1:], field[:, -1:]], axis=0)
    west_rim = passed_along(west_column, "lon", 1)[:, 0]
    paired = field.reshape(half_rows, 2, half_cols, 2 * depth)
    even_rows = paired[:, 0]
    odd_rows = paired[:, 1]
    upper_paired = upper_rim.reshape(1, half_cols, 2 * depth)
    above_rows = jnp.concatenate([upper_paired, odd_rows[:-1]], axis=0)
    tap_rows = (above_rows, even_rows, odd_rows)
    zero_block = jnp.zeros((depth, depth), kernel.dtype)
    summed = jnp.zeros((half_rows * half_cols, 2 * depth), jnp.float32)
    west_sum = jnp.zeros((half_rows, depth), jnp.float32)
    for row_tap in range(3):
        upper_half = jnp.concatenate([kernel[row_tap, 1], zero_block], axis=1)
        lower_half = jnp.concatenate([kernel[row_tap, 2], kernel[row_tap, 0]], axis=1)
        stacked = jnp.concatenate([upper_half, lower_half], axis=0)
        rows_flat = tap_rows[row_tap].reshape(-1, 2 * depth)
        summed = summed + jnp.dot(rows_flat, stacked, preferred_element_type=jnp.float32)
        west_rows = west_rim[row_tap : row_tap + height : 2]
        west_sum = west_sum + jnp.dot(
            west_rows, kernel[row_tap, 0], preferred_element_type=jnp.float32
        )
    summed = summed.reshape(half_rows, half_cols, 2 * depth)
    central = summed[:, :, :depth]
    westward = summed[:, :, depth:]
    shifted = jnp.concatenate([west_sum[:, None, :], westward[:, :-1]], axis=1)
    return central + shifted


def body(
    radiances,
    project_weight,
    tile_ids,
    slot_offsets,
    tile_counts,
    setconv_weights,
    conv1_weight,
    conv2_weight,
):
    lat_size = lax.axis_size("lat")
    lon_size = lax.axis_size("lon")
    peer_count = lat_size * lon_size
    obs_count = radiances.shape[0]
    capacity = 7 * (obs_count // peer_count) // 2
    slot_count = setconv_weights.shape[2]
    channel_count = project_weight.shape[1]
    targets = jnp.arange(peer_count, dtype=jnp.int32)
    row_index = jnp.arange(obs_count, dtype=jnp.int32)
    matches = tile_ids[:, None] == targets[None, :]
    run_counts = jnp.sum(matches.astype(jnp.int32), axis=0)
    run_starts = jnp.min(jnp.where(matches, row_index[:, None], obs_count), axis=0)
    within = jnp.arange(capacity, dtype=jnp.int32)
    source_rows = jnp.minimum(run_starts[:, None] + within[None, :], obs_count - 1).reshape(-1)
    valid_slot = (within[None, :] < run_counts[:, None]).reshape(-1)
    payload = jnp.dot(radiances, project_weight, preferred_element_type=jnp.float32).astype(
        jnp.bfloat16
    )
    row_width = payload.shape[1]
    packed = jnp.where(
        valid_slot[:, None], jnp.take(payload, source_rows, axis=0), jnp.zeros((), jnp.bfloat16)
    )
    offsets_out = jnp.where(valid_slot, jnp.take(slot_offsets, source_rows, axis=0), slot_count)
    arrived, arrived_offsets = (
        lax.all_to_all(
            packed.reshape(peer_count, capacity, row_width),
            ("lat", "lon"),
            split_axis=0,
            concat_axis=0,
            tiled=True,
        ),
        lax.all_to_all(
            offsets_out.reshape(peer_count, capacity),
            ("lat", "lon"),
            split_axis=0,
            concat_axis=0,
            tiled=True,
        ),
    )
    arrived = arrived.reshape(-1, row_width)
    arrived_offsets = arrived_offsets.reshape(-1)
    slot_table = (
        jnp.arange(slot_count, dtype=jnp.int32)[:, None] == arrived_offsets[None, :]
    ).astype(jnp.bfloat16)
    obs_block = jnp.dot(slot_table, arrived, preferred_element_type=jnp.float32).astype(
        jnp.bfloat16
    )
    tile_rows, tile_cols = (setconv_weights.shape[0], setconv_weights.shape[1])
    weights_flat = setconv_weights.reshape(-1, slot_count)
    live_mask = jnp.arange(slot_count, dtype=jnp.int32) < tile_counts.reshape(-1)[0]
    masked = jnp.where(live_mask[None, :], weights_flat, jnp.zeros((), jnp.bfloat16))
    numerator = jnp.dot(masked, obs_block, preferred_element_type=jnp.float32)
    density = jnp.sum(masked, axis=1, dtype=jnp.float32)
    grid = (
        (numerator / jnp.sqrt(density)[:, None])
        .astype(jnp.bfloat16)
        .reshape(tile_rows, tile_cols, channel_count)
    )
    hidden = jax.nn.gelu(stride_conv(grid, conv1_weight)).astype(jnp.bfloat16)
    return stride_conv(hidden, conv2_weight).astype(jnp.bfloat16)


def solution(mesh):
    in_specs = (
        P(("lat", "lon"), None),
        P(),
        P(("lat", "lon")),
        P(("lat", "lon")),
        P("lat", "lon"),
        P("lat", "lon", None),
        P(),
        P(),
    )
    out_specs = P("lat", "lon", None)
    return jax.shard_map(body, mesh=mesh, in_specs=in_specs, out_specs=out_specs, check_vma=False)
```

profile of v0, /device:TPU:17, one launch (start us, length us, event | category | flops | bytes accessed | tf_op | source)
XLA Modules:
  0.0 142.2 jit_solution(7751144918593287627)
XLA Ops:
  0.0 0.8 convert_reduce_fusion.1
  1.1 12.9 %gather_fusion = s32[3584]{0:T(1024)S(1)} fusion(s32[1024]{0:T(1024)S(1)} %copy-done, s32[4096]{0:T(1024)S(1)} %pad_clamp_fusion), kind=kCustom, calls=%fused_computation | custom fusion | bytes 43008 | tf_op jit(solution)/shard_map/jit(_take)/gather | solution.py:83
  14.1 0.7 compare_select_fusion.2
  14.9 6.2 %all-to-all-start = ((s32[32,1,112]{2,1,0:T(1,128)}), s32[32,1,112]{2,1,0:T(1,128)S(1)}, u32[]{:S(2)}, u32[]{:S(2)}) async-start(s32[32,1,112]{2,1,0:T(1,128)} %compare_select_fusion.2), calls=%async_computation | async-start | bytes 32768 | tf_op jit(solution)/shard_map/all_to_all | solution.py:92
  21.2 12.0 %convolution_convert_fusion = bf16[1024,256]{1,0:T(8,128)(2,1)S(1)} fusion(bf16[1024,8461]{0,1:T(8,128)(2,1)} %param.8, bf16[8461,256]{1,0:T(8,128)(2,1)} %param.9), kind=kOutput, calls=%fused_computation.13 | convolution fusion | flops 4436262912 | bytes 22184448 | tf_op jit(solution)/shard_map/dot_general | solution.py:76
  33.2 10.4 %gather_fusion.1 = bf16[3584,256]{1,0:T(8,128)(2,1)S(1)} fusion(bf16[1024,256]{1,0:T(8,128)(2,1)S(1)} %convolution_convert_fusion, s32[4096]{0:T(1024)S(1)} %pad_clamp_fusion), kind=kCustom, calls=%fused_computation.1 | custom fusion | bytes 3684352 | tf_op jit(solution)/shard_map/jit(_take)/gather | solution.py:81
  43.6 2.5 %select_select_fusion = bf16[32,112,256]{2,1,0:T(8,128)(2,1)} fusion(bf16[32,112,256]{2,1,0:T(8,128)(2,1)S(1)} %bitcast.96, pred[32,112]{1,0:T(8,128)(4,1)S(1)} %get-tuple-element.28, pred[32,112]{1,0:T(8,128)(4,1)S(1)} %get-tuple-element.27), kind=kLoop, calls=%fused_computation.10 | loop fusion | flops 1835008 | bytes 3677184 | tf_op jit(solution)/shard_map/jit(_where)/select_n | solution.py:80
  46.1 5.9 %all-to-all-start.1 = ((bf16[32,112,256]{2,1,0:T(8,128)(2,1)}), bf16[32,112,256]{2,1,0:T(8,128)(2,1)}, u32[]{:S(2)}, u32[]{:S(2)}) async-start(bf16[32,112,256]{2,1,0:T(8,128)(2,1)} %select_select_fusion), calls=%async_computation.1 | async-start | bytes 3670016 | tf_op jit(solution)/shard_map/all_to_all | solution.py:85
  52.7 6.4 %convert_reduce_fusion = f32[64,32]{1,0:T(8,128)S(1)} fusion(bf16[64,32,2560]{2,1,0:T(8,128)(2,1)} %param.13, pred[2560]{0:T(1024)(128)(4,1)S(1)} %iota_compare_fusion.7), kind=kLoop, calls=%fused_computation.4 | loop fusion | flops 15726592 | bytes 10496512 | tf_op jit(solution)/shard_map/reduce_sum | solution.py:113
  59.2 1.0 slice_bitcast_fusion.15
  60.8 1.0 slice_bitcast_fusion.6
  61.7 9.9 %bitcast_select_fusion = bf16[2048,2560]{1,0:T(8,128)(2,1)} fusion(bf16[64,32,2560]{2,1,0:T(8,128)(2,1)} %param.13, pred[2560]{0:T(1024)(128)(4,1)S(1)} %iota_compare_fusion.7), kind=kLoop, calls=%fused_computation.6 | loop fusion | flops 5242880 | bytes 20974080 | tf_op jit(solution)/shard_map/jit(_where)/select_n | solution.py:111
  73.6 20.3 %all-to-all-done.1 = bf16[32,112,256]{2,1,0:T(8,128)(2,1)} async-done(((bf16[32,112,256]{2,1,0:T(8,128)(2,1)}), bf16[32,112,256]{2,1,0:T(8,128)(2,1)}, u32[]{:S(2)}, u32[]{:S(2)}) %all-to-all-start.1) | async-done | bytes 1835040 | tf_op jit(solution)/shard_map/all_to_all | solution.py:85
  93.9 18.0 %fusion.3 = bf16[2048,256]{1,0:T(8,128)(2,1)S(1)} fusion(bf16[2048,2560]{1,0:T(8,128)(2,1)} %bitcast_select_fusion, f32[2048]{0:T(1024)S(1)} %sqrt.11, bf16[3584,256]{1,0:T(8,128)(2,1)} %bitcast.3, s32[3584]{0:T(1024)} %eq.32), kind=kOutput, calls=%fused_computation.9 | convolution fusion | flops 7392854016 | bytes 13391872 | tf_op jit(solution)/shard_map/dot_general | solution.py:112
  111.9 1.0 copy-done.3
  113.5 1.4 reshape_reshape.3
  114.9 2.7 %collective-permute-start = (bf16[1,32,256]{2,1,0:T(8,128)(2,1)}, bf16[1,32,256]{2,1,0:T(8,128)(2,1)S(1)}, u32[]{:S(2)}, u32[]{:S(2)}) collective-permute-start(bf16[1,32,256]{2,1,0:T(8,128)(2,1)} %slice_bitcast_fusion.24), channel_id=1, source_target_pairs={{0,8},{8,16},{16,24},{1,9},{9,17},{17,25},{2,10},{10,18},{18,26},{... | collective-permute-start | bytes 49160 | tf_op jit(solution)/shard_map/ppermute | solution.py:10
  117.7 0.9 fusion.99
  118.6 1.4 fusion.26
  120.0 0.8 slice_bitcast_fusion
  120.8 1.0 slice.194
  122.5 1.4 %collective-permute-start.1 = (bf16[65,1,256]{2,0,1:T(8,128)(2,1)}, bf16[65,1,256]{2,0,1:T(8,128)(2,1)}, u32[]{:S(2)}, u32[]{:S(2)}) collective-permute-start(bf16[65,1,256]{2,0,1:T(8,128)(2,1)} %pad_maximum_fusion.1), channel_id=1, source_target_pairs={{0,1},{1,2},{2,3},{3,4},{4,5},{5,6},{6,7},{7,0},{8,9},{9,10},{10,1... | collective-permute-start | bytes 99848 | tf_op jit(solution)/shard_map/ppermute | solution.py:16
  124.7 1.1 pad_maximum_fusion
  125.8 1.9 %convolution_add_fusion.1 = f32[512,512]{1,0:T(8,128)S(1)} fusion(f32[512,512]{1,0:T(8,128)} %fusion.26, bf16[512,512]{1,0:T(8,128)(2,1)S(1)} %bitcast.100, bf16[256,256]{1,0:T(8,128)(2,1)} %get-tuple-element.23, bf16[256,256]{1,0:T(8,128)(2,1)} %get-tuple-element.21, bf16[256,256]{1,0:T(8,128)(2,1)} %get-tuple-element.22), kind=kOutput, calls=%fused_computation.12 | convolution fusion | flops 270794752 | bytes 3014656 | tf_op jit(solution)/shard_map/dot_general | solution.py:39
  128.6 0.8 slice.160
  129.4 0.8 slice.161
  130.2 1.4 slice.159
  131.8 0.9 fusion.6
  133.4 1.9 %collective-permute-start.2 = (bf16[1,16,256]{2,0,1:T(2,128)(2,1)S(1)}, bf16[1,16,256]{2,0,1:T(2,128)(2,1)S(1)}, u32[]{:S(2)}, u32[]{:S(2)}) collective-permute-start(bf16[1,16,256]{2,0,1:T(2,128)(2,1)S(1)} %slice.196), channel_id=1, source_target_pairs={{0,8},{8,16},{16,24},{1,9},{9,17},{17,25},{2,10},{10,18},{18,26},{... | collective-permute-start | bytes 24584 | tf_op jit(solution)/shard_map/ppermute | solution.py:10
  135.4 2.5 %collective-permute-done.2 = bf16[1,16,256]{2,0,1:T(2,128)(2,1)S(1)} collective-permute-done((bf16[1,16,256]{2,0,1:T(2,128)(2,1)S(1)}, bf16[1,16,256]{2,0,1:T(2,128)(2,1)S(1)}, u32[]{:S(2)}, u32[]{:S(2)}) %collective-permute-start.2) | collective-permute-done | bytes 8224 | tf_op jit(solution)/shard_map/ppermute | solution.py:10
  137.9 1.2 collective-permute-start.3
  139.1 1.3 fusion.31
  (81 shorter events, 8.5 us)
Async XLA Ops:
  0.0 1.1 copy-start
  14.9 31.2 %all-to-all-start = ((s32[32,1,112]{2,1,0:T(1,128)}), s32[32,1,112]{2,1,0:T(1,128)S(1)}, u32[]{:S(2)}, u32[]{:S(2)}) async-start(s32[32,1,112]{2,1,0:T(1,128)} %compare_select_fusion.2), calls=%async_computation | async-start | bytes 32768 | tf_op jit(solution)/shard_map/all_to_all | solution.py:92
  46.1 47.7 %all-to-all-start.1 = ((bf16[32,112,256]{2,1,0:T(8,128)(2,1)}), bf16[32,112,256]{2,1,0:T(8,128)(2,1)}, u32[]{:S(2)}, u32[]{:S(2)}) async-start(bf16[32,112,256]{2,1,0:T(8,128)(2,1)} %select_select_fusion), calls=%async_computation.1 | async-start | bytes 3670016 | tf_op jit(solution)/shard_map/all_to_all | solution.py:85
  52.7 6.5 %copy-start.1 = (bf16[3,3,256,256]{3,2,1,0:T(8,128)(2,1)S(1)}, bf16[3,3,256,256]{3,2,1,0:T(8,128)(2,1)}, u32[]{:S(2)}) copy-start(bf16[3,3,256,256]{3,2,1,0:T(8,128)(2,1)} %param.14) | copy-start | bytes 3538948
  59.1 1.7 %copy-start.2 = (bf16[3,3,256,256]{3,2,1,0:T(8,128)(2,1)S(1)}, bf16[3,3,256,256]{3,2,1,0:T(8,128)(2,1)}, u32[]{:S(2)}) copy-start(bf16[3,3,256,256]{3,2,1,0:T(8,128)(2,1)} %param.15) | copy-start | bytes 3538948
  111.9 1.0 copy-start.3
  114.9 3.7 %copy-start.13 = (bf16[256,256]{1,0:T(8,128)(2,1)S(1)}, bf16[256,256]{1,0:T(8,128)(2,1)}, u32[]{:S(2)}) copy-start(bf16[256,256]{1,0:T(8,128)(2,1)} %get-tuple-element.18) | copy-start | bytes 393220
  114.9 3.7 %copy-start.14 = (bf16[256,256]{1,0:T(8,128)(2,1)S(1)}, bf16[256,256]{1,0:T(8,128)(2,1)}, u32[]{:S(2)}) copy-start(bf16[256,256]{1,0:T(8,128)(2,1)} %get-tuple-element.19) | copy-start | bytes 393220
  114.9 3.6 %copy-start.15 = (bf16[256,256]{1,0:T(8,128)(2,1)S(1)}, bf16[256,256]{1,0:T(8,128)(2,1)}, u32[]{:S(2)}) copy-start(bf16[256,256]{1,0:T(8,128)(2,1)} %get-tuple-element.20) | copy-start | bytes 393220
  114.9 6.9 %collective-permute-start = (bf16[1,32,256]{2,1,0:T(8,128)(2,1)}, bf16[1,32,256]{2,1,0:T(8,128)(2,1)S(1)}, u32[]{:S(2)}, u32[]{:S(2)}) collective-permute-start(bf16[1,32,256]{2,1,0:T(8,128)(2,1)} %slice_bitcast_fusion.24), channel_id=1, source_target_pairs={{0,8},{8,16},{16,24},{1,9},{9,17},{17,25},{2,10},{10,18},{18,26},{... | collective-permute-start | bytes 49160 | tf_op jit(solution)/shard_map/ppermute | solution.py:10
  121.9 0.7 copy-start.16
  122.5 6.1 %collective-permute-start.1 = (bf16[65,1,256]{2,0,1:T(8,128)(2,1)}, bf16[65,1,256]{2,0,1:T(8,128)(2,1)}, u32[]{:S(2)}, u32[]{:S(2)}) collective-permute-start(bf16[65,1,256]{2,0,1:T(8,128)(2,1)} %pad_maximum_fusion.1), channel_id=1, source_target_pairs={{0,1},{1,2},{2,3},{3,4},{4,5},{5,6},{6,7},{7,0},{8,9},{9,10},{10,1... | collective-permute-start | bytes 99848 | tf_op jit(solution)/shard_map/ppermute | solution.py:16
  125.8 2.0 %copy-start.4 = (bf16[32,1,16,512]{3,2,1,0:T(8,128)(2,1)S(1)}, bf16[32,1,16,512]{3,2,1,0:T(8,128)(2,1)}, u32[]{:S(2)}) copy-start(bf16[32,1,16,512]{3,2,1,0:T(8,128)(2,1)} %get-tuple-element.25) | copy-start | bytes 1572868
  125.8 2.0 %copy-start.10 = (bf16[256,256]{1,0:T(8,128)(2,1)S(1)}, bf16[256,256]{1,0:T(8,128)(2,1)}, u32[]{:S(2)}) copy-start(bf16[256,256]{1,0:T(8,128)(2,1)} %get-tuple-element.16) | copy-start | bytes 393220
  125.8 2.0 %copy-start.11 = (bf16[256,256]{1,0:T(8,128)(2,1)S(1)}, bf16[256,256]{1,0:T(8,128)(2,1)}, u32[]{:S(2)}) copy-start(bf16[256,256]{1,0:T(8,128)(2,1)} %get-tuple-element.17) | copy-start | bytes 393220
  125.8 2.0 %copy-start.12 = (bf16[256,256]{1,0:T(8,128)(2,1)S(1)}, bf16[256,256]{1,0:T(8,128)(2,1)}, u32[]{:S(2)}) copy-start(bf16[256,256]{1,0:T(8,128)(2,1)} %get-tuple-element.24) | copy-start | bytes 393220
  133.2 7.3 %copy-start.7 = (bf16[256,256]{1,0:T(8,128)(2,1)S(1)}, bf16[256,256]{1,0:T(8,128)(2,1)}, u32[]{:S(2)}) copy-start(bf16[256,256]{1,0:T(8,128)(2,1)} %get-tuple-element.9) | copy-start | bytes 393220
  133.2 7.3 %copy-start.8 = (bf16[256,256]{1,0:T(8,128)(2,1)S(1)}, bf16[256,256]{1,0:T(8,128)(2,1)}, u32[]{:S(2)}) copy-start(bf16[256,256]{1,0:T(8,128)(2,1)} %get-tuple-element.10) | copy-start | bytes 393220
  133.2 7.3 %copy-start.9 = (bf16[256,256]{1,0:T(8,128)(2,1)S(1)}, bf16[256,256]{1,0:T(8,128)(2,1)}, u32[]{:S(2)}) copy-start(bf16[256,256]{1,0:T(8,128)(2,1)} %get-tuple-element.11) | copy-start | bytes 393220
  133.4 4.5 %collective-permute-start.2 = (bf16[1,16,256]{2,0,1:T(2,128)(2,1)S(1)}, bf16[1,16,256]{2,0,1:T(2,128)(2,1)S(1)}, u32[]{:S(2)}, u32[]{:S(2)}) collective-permute-start(bf16[1,16,256]{2,0,1:T(2,128)(2,1)S(1)} %slice.196), channel_id=1, source_target_pairs={{0,8},{8,16},{16,24},{1,9},{9,17},{17,25},{2,10},{10,18},{18,26},{... | collective-permute-start | bytes 24584 | tf_op jit(solution)/shard_map/ppermute | solution.py:10
  137.9 3.1 %collective-permute-start.3 = (bf16[33,1,256]{2,0,1:T(8,128)(2,1)S(1)}, bf16[33,1,256]{2,0,1:T(8,128)(2,1)S(1)}, u32[]{:S(2)}, u32[]{:S(2)}) collective-permute-start(bf16[33,1,256]{2,0,1:T(8,128)(2,1)S(1)} %pad_maximum_fusion.2), channel_id=1, source_target_pairs={{0,1},{1,2},{2,3},{3,4},{4,5},{5,6},{6,7},{7,0},{8,9},{9,10},{10,1... | collective-permute-start | bytes 50696 | tf_op jit(solution)/shard_map/ppermute | solution.py:16
  139.1 1.6 %copy-start.5 = (bf16[256,256]{1,0:T(8,128)(2,1)S(1)}, bf16[256,256]{1,0:T(8,128)(2,1)}, u32[]{:S(2)}) copy-start(bf16[256,256]{1,0:T(8,128)(2,1)} %get-tuple-element.8) | copy-start | bytes 393220
  139.1 1.6 %copy-start.6 = (bf16[256,256]{1,0:T(8,128)(2,1)S(1)}, bf16[256,256]{1,0:T(8,128)(2,1)}, u32[]{:S(2)}) copy-start(bf16[256,256]{1,0:T(8,128)(2,1)} %get-tuple-element.15) | copy-start | bytes 393220
where the time goes:
time: 145 us; the launch traced here: 142 us
  local copies, waits for them, and re-layouts  37.7 us (26%)
  matrix products  37 us (26%)
  other arithmetic  24.2 us (17%)
  waiting for transfers between devices  22.8 us (16%)
  starting transfers between devices  19.4 us (13%)
    all_to_all x1, waiting for transfers between devices, body(): lax.all_to_all(packed.reshape(peer_count, capacity, row_width), ('lat', '...  20.3 us
    dot_general x1, matrix products, body(): numerator = jnp.dot(masked, obs_block, preferred_element_type=jnp.float32)  18 us
    gather x2, local copies, waits for them, and re-layouts, body(): jnp.take(slot_offsets, source_rows, axis=0)  13 us
    dot_general x1, matrix products, body(): jnp.dot(radiances, project_weight, preferred_element_type=jnp.float32)  12 us
    gather x1, local copies, waits for them, and re-layouts, body(): jnp.take(payload, source_rows, axis=0)  10.4 us
    select_n x1, other arithmetic, body(): jnp.where(live_mask[None, :], weights_flat, jnp.zeros((), jnp.bfloat16))  9.95 us
    reduce_sum x1, other arithmetic, body(): density = jnp.sum(masked, axis=1, dtype=jnp.float32)  6.38 us
    all_to_all x1, starting transfers between devices, body(): lax.all_to_all(offsets_out.reshape(peer_count, capacity), ('lat', 'lon'),...  6.25 us
  transfers between devices with their start and end apart: 6, of which 2 were waited for; matrix products, arithmetic and copies ran while one was open for 39% of the time, Pallas kernels for 0%

commit v1 on v0

v1 whole, which is shorter than its diff:
```python
import functools

import jax
import jax.numpy as jnp
from jax import lax
from jax.experimental import pallas as pl
from jax.experimental.pallas import tpu as pltpu
from jax.sharding import PartitionSpec as P

MESH = pl.DeviceIdType.MESH
MIB = 1024 * 1024


def project_pack_kernel(steps, rows, rad_ref, weight_ref, pos_ref, packed_ref, feat_ref):
    step = pl.program_id(0)
    feat_ref[pl.ds(pl.multiple_of(step * rows, rows), rows), :] = jnp.dot(
        rad_ref[...], weight_ref[...], preferred_element_type=jnp.float32
    ).astype(jnp.bfloat16)

    @pl.when(step == steps - 1)
    def _():
        total = packed_ref.shape[0]
        chunk = 256 if total % 256 == 0 else 128
        obs = feat_ref.shape[0]

        @pl.loop(0, total // chunk)
        def _(c):
            base = pl.multiple_of(c * chunk, chunk)
            target = lax.broadcasted_iota(jnp.int32, (chunk, obs), 0) + base
            onehot = (target == pos_ref[...]).astype(jnp.float32).astype(jnp.bfloat16)
            packed_ref[pl.ds(base, chunk), :] = jnp.dot(
                onehot, feat_ref[...], preferred_element_type=jnp.float32
            ).astype(jnp.bfloat16)


def project_pack(radiances, weight, pos, total):
    obs, raw = radiances.shape
    channels = weight.shape[1]
    rows = 256
    steps = obs // rows
    return pl.pallas_call(
        functools.partial(project_pack_kernel, steps, rows),
        grid=(steps,),
        out_shape=jax.ShapeDtypeStruct((total, channels), jnp.bfloat16),
        in_specs=[
            pl.BlockSpec((rows, raw), lambda i: (i, 0)),
            pl.BlockSpec((raw, channels), lambda i: (0, 0)),
            pl.BlockSpec((1, obs), lambda i: (0, 0)),
        ],
        out_specs=pl.BlockSpec((total, channels), lambda i: (0, 0)),
        scratch_shapes=[pltpu.VMEM((obs, channels), jnp.bfloat16)],
        compiler_params=pltpu.CompilerParams(vmem_limit_bytes=48 * MIB),
        cost_estimate=pl.CostEstimate(
            flops=2 * obs * raw * channels,
            bytes_accessed=2 * (obs * raw + raw * channels + total * channels),
            transcendentals=0,
        ),
        name="project_pack",
    )(radiances, weight, pos)


def setconv_kernel(
    n_lat, n_lon, cap, group, chunk,
    packed_ref, slots_ref, live_ref, w_hbm, out_ref,
    arrived, w_vmem, obs, dens, send_sem, recv_sem, own_sem, w_sem,
):
    n = n_lat * n_lon
    me = lax.axis_index("lat") * n_lon + lax.axis_index("lon")
    cells, slot_count = w_vmem.shape
    chunks = cells // chunk

    def w_copy(c):
        part = pl.ds(pl.multiple_of(c * chunk, chunk), chunk)
        return pltpu.make_async_copy(w_hbm.at[part], w_vmem.at[part], w_sem.at[c])

    def send(d):
        peer = lax.rem(me + d, n)
        return pltpu.make_async_remote_copy(
            src_ref=packed_ref.at[peer],
            dst_ref=arrived.at[me],
            send_sem=send_sem.at[d],
            recv_sem=recv_sem.at[me],
            device_id=(peer // n_lon, lax.rem(peer, n_lon)),
            device_id_type=MESH,
        )

    def arrival(source):
        return pltpu.make_async_remote_copy(
            src_ref=packed_ref.at[source],
            dst_ref=arrived.at[source],
            send_sem=send_sem.at[0],
            recv_sem=recv_sem.at[source],
            device_id=(source // n_lon, lax.rem(source, n_lon)),
            device_id_type=MESH,
        )

    barrier = pltpu.get_barrier_semaphore()

    @pl.loop(1, n)
    def _(d):
        peer = lax.rem(me + d, n)
        pl.semaphore_signal(
            barrier, inc=1, device_id=(peer // n_lon, lax.rem(peer, n_lon)), device_id_type=MESH
        )

    own = pltpu.make_async_copy(packed_ref.at[me], arrived.at[me], own_sem)
    own.start()
    pl.semaphore_wait(barrier, n - 1)

    @pl.loop(1, n)
    def _(d):
        send(d).start()

    @pl.loop(0, chunks)
    def _(c):
        w_copy(c).start()

    obs[...] = jnp.zeros_like(obs)

    @pl.loop(0, chunks)
    def _(c):
        w_copy(c).wait()
        part = pl.ds(pl.multiple_of(c * chunk, chunk), chunk)
        dens[part, :] = jnp.dot(
            w_vmem[part, :], live_ref[...], preferred_element_type=jnp.float32
        )

    own.wait()
    width = group * cap
    groups = n // group
    obs_chunk = 256

    @pl.loop(0, groups)
    def _(k):
        g = lax.rem(me // group + k, groups)
        for j in range(group):
            source = g * group + j

            @pl.when(source != me)
            def _():
                arrival(source).wait_recv()

        rows = arrived[pl.ds(g * group, group)].reshape(width, arrived.shape[2])
        slots = slots_ref[g]

        @pl.loop(0, slot_count // obs_chunk)
        def _(c):
            base = pl.multiple_of(c * obs_chunk, obs_chunk)
            at = lax.broadcasted_iota(jnp.int32, (obs_chunk, width), 0) + base
            onehot = (at == slots).astype(jnp.float32).astype(jnp.bfloat16)
            placed = jnp.dot(onehot, rows, preferred_element_type=jnp.float32)
            obs[pl.ds(base, obs_chunk), :] += placed.astype(jnp.bfloat16)

    @pl.loop(0, chunks)
    def _(c):
        part = pl.ds(pl.multiple_of(c * chunk, chunk), chunk)
        numerator = jnp.dot(w_vmem[part, :], obs[...], preferred_element_type=jnp.float32)
        root = jnp.sqrt(dens[part, :])
        root = jnp.concatenate([root] * (numerator.shape[1] // root.shape[1]), axis=1)
        out_ref[part, :] = (numerator / root).astype(jnp.bfloat16)

    @pl.loop(1, n)
    def _(d):
        send(d).wait_send()


def setconv(packed, slots, live, weights, n_lat, n_lon, cap, group):
    n = n_lat * n_lon
    channels = packed.shape[2]
    cells, slot_count = weights.shape
    chunk = 256
    vmem = pl.BlockSpec(memory_space=pltpu.VMEM)
    return pl.pallas_call(
        functools.partial(setconv_kernel, n_lat, n_lon, cap, group, chunk),
        out_shape=jax.ShapeDtypeStruct((cells, channels), jnp.bfloat16),
        in_specs=[vmem, vmem, vmem, pl.BlockSpec(memory_space=pl.ANY)],
        out_specs=vmem,
        scratch_shapes=[
            pltpu.VMEM((n, cap, channels), jnp.bfloat16),
            pltpu.VMEM((cells, slot_count), jnp.bfloat16),
            pltpu.VMEM((slot_count, channels), jnp.bfloat16),
            pltpu.VMEM((cells, 128), jnp.float32),
            pltpu.SemaphoreType.DMA((n,)),
            pltpu.SemaphoreType.DMA((n,)),
            pltpu.SemaphoreType.DMA,
            pltpu.SemaphoreType.DMA((cells // chunk,)),
        ],
        compiler_params=pltpu.CompilerParams(
            collective_id=0, has_side_effects=True, vmem_limit_bytes=48 * MIB
        ),
        cost_estimate=pl.CostEstimate(
            flops=4 * cells * slot_count * channels,
            bytes_accessed=2 * cells * slot_count,
            transcendentals=0,
        ),
        name="setconv",
    )(packed, slots, live, weights)


def load_rows(ref, rows):
    return jnp.concatenate([ref[h, rows, :] for h in range(ref.shape[0])], axis=1)


def store_rows(ref, rows, value):
    for h in range(ref.shape[0]):
        ref[h, rows, :] = value[:, h * 128:(h + 1) * 128]


def conv_stage(first, n_lat, n_lon, lat, lon, field, weight, height, width,
               even, odd, column, west, corner, shift, sems):
    half = width // 2
    depth = even.shape[2]
    pairs = height * half
    even[1:, :, :] = load_rows(field, pl.ds(0, pairs, stride=2)).reshape(height, half, depth)
    odd[1:, :, :] = load_rows(field, pl.ds(1, pairs, stride=2)).reshape(height, half, depth)
    store_rows(column, pl.ds(0, height), load_rows(field, pl.ds(width - 1, height, stride=width)))
    below = lax.rem(lat + 1, n_lat)
    east = lax.rem(lon + 1, n_lon)

    def copy(src, dst, k, device):
        return pltpu.make_async_remote_copy(
            src_ref=src, dst_ref=dst, send_sem=sems.at[0, first + k],
            recv_sem=sems.at[1, first + k], device_id=device, device_id_type=MESH,
        )

    sideways = copy(column, west.at[:, pl.ds(8, height)], 0, (lat, east))
    downward = [
        copy(odd.at[height], odd.at[0], 1, (below, lon)),
        copy(even.at[height], even.at[0], 2, (below, lon)),
        copy(odd.at[height], corner, 3, (below, east)),
    ]

    @pl.when(lat < n_lat - 1)
    def _():
        for item in downward:
            item.start()

    sideways.start()

    @pl.when(lat == 0)
    def _():
        even[0] = jnp.zeros_like(even[0])
        odd[0] = jnp.zeros_like(odd[0])
        corner[...] = jnp.zeros_like(corner)

    out_rows = height // 2
    flat = out_rows * half

    def rows_of(ref, tap):
        start = 1 if tap else 0
        picked = ref[start:start + 2 * out_rows].reshape(out_rows, 2, half, depth)
        return picked[:, tap - start].reshape(flat, depth).astype(jnp.bfloat16)

    def dot(rows, a, b):
        return jnp.dot(rows, weight[a, b], preferred_element_type=jnp.float32)

    central = None
    westward = None
    for tap in (1, 2, 0):
        if tap == 0:
            @pl.when(lat > 0)
            def _():
                for item in downward:
                    item.wait_recv()
        odd_rows = rows_of(odd, tap)
        c = dot(rows_of(even, tap), tap, 1) + dot(odd_rows, tap, 2)
        w = dot(odd_rows, tap, 0)
        central = c if central is None else central + c
        westward = w if westward is None else westward + w
    store_rows(shift, pl.ds(8, flat), westward)
    sideways.wait_recv()
    store_rows(west, pl.ds(7, 1), corner[half - 1:half, :])
    rim = jnp.zeros((out_rows, depth), jnp.float32)
    for tap in range(3):
        taken = load_rows(west, pl.ds(7 + tap, out_rows, stride=2)).astype(jnp.bfloat16)
        rim = rim + dot(taken, tap, 0)
    store_rows(shift, pl.ds(7, out_rows, stride=half), rim)
    result = central + load_rows(shift, pl.ds(7, flat))

    @pl.when(lat < n_lat - 1)
    def _():
        for item in downward:
            item.wait_send()

    sideways.wait_send()
    return result


def encode_kernel(
    n_lat, n_lon, height, width, grid_ref, k1_ref, k2_ref, out_ref,
    field1, even1, odd1, col1, west1, corner1, shift1,
    field2, even2, odd2, col2, west2, corner2, shift2, sems,
):
    lat = lax.axis_index("lat")
    lon = lax.axis_index("lon")
    barrier = pltpu.get_barrier_semaphore()
    below = lax.rem(lat + 1, n_lat)
    above = lax.rem(lat + n_lat - 1, n_lat)
    east = lax.rem(lon + 1, n_lon)
    west = lax.rem(lon + n_lon - 1, n_lon)
    peers = [(lat, east), (lat, west), (below, lon), (above, lon), (below, east), (above, west)]
    for peer in peers:
        pl.semaphore_signal(barrier, inc=1, device_id=peer, device_id_type=MESH)
    store_rows(field1, pl.ds(0, height * width), grid_ref[...].astype(jnp.float32))
    pl.semaphore_wait(barrier, len(peers))
    first = conv_stage(0, n_lat, n_lon, lat, lon, field1, k1_ref, height, width,
                       even1, odd1, col1, west1, corner1, shift1, sems)
    hidden = jax.nn.gelu(first).astype(jnp.bfloat16)
    store_rows(field2, pl.ds(0, height * width // 4), hidden.astype(jnp.float32))
    second = conv_stage(4, n_lat, n_lon, lat, lon, field2, k2_ref, height // 2, width // 2,
                        even2, odd2, col2, west2, corner2, shift2, sems)
    out_ref[...] = second.astype(jnp.bfloat16)


def encode(grid, kernel1, kernel2, n_lat, n_lon, height, width):
    depth = grid.shape[1]
    vmem = pl.BlockSpec(memory_space=pltpu.VMEM)

    def scratch(h, w):
        f32 = lambda *shape: pltpu.VMEM(shape, jnp.float32)
        lanes = depth // 128
        return [
            f32(lanes, h * w, 128), f32(h + 1, w // 2, depth), f32(h + 1, w // 2, depth),
            f32(lanes, h, 128), f32(lanes, h + 8, 128), f32(w // 2, depth),
            f32(lanes, h * w // 4 + 8, 128),
        ]

    return pl.pallas_call(
        functools.partial(encode_kernel, n_lat, n_lon, height, width),
        out_shape=jax.ShapeDtypeStruct((height * width // 16, depth), jnp.bfloat16),
        in_specs=[vmem] * 3,
        out_specs=vmem,
        scratch_shapes=scratch(height, width) + scratch(height // 2, width // 2)
        + [pltpu.SemaphoreType.DMA((2, 8))],
        compiler_params=pltpu.CompilerParams(
            collective_id=1, has_side_effects=True, vmem_limit_bytes=48 * MIB
        ),
        name="encode",
    )(grid, kernel1, kernel2)


def body(
    radiances, project_weight, tile_ids, slot_offsets, tile_counts,
    setconv_weights, conv1_weight, conv2_weight,
):
    n_lat = lax.axis_size("lat")
    n_lon = lax.axis_size("lon")
    n = n_lat * n_lon
    obs_count = radiances.shape[0]
    limit = 7 * (obs_count // n) // 2
    cap = -(-limit // 16) * 16
    group = max(1, 256 // cap)
    tile_rows, tile_cols, slot_count = setconv_weights.shape
    channels = project_weight.shape[1]

    place = jnp.arange(obs_count, dtype=jnp.int32) % cap
    pos = (tile_ids * cap + place).reshape(1, obs_count)
    keys = lax.all_gather(tile_ids * 4096 + slot_offsets, ("lat", "lon"))
    packed = project_pack(radiances, project_weight, pos, n * cap)

    me = lax.axis_index("lat") * n_lon + lax.axis_index("lon")
    turns = -(-obs_count // cap)
    keys = jnp.pad(keys, ((0, 0), (0, turns * cap - obs_count)), constant_values=-1)
    keys = keys.reshape(n, turns, cap)
    slots = jnp.max(jnp.where(keys // 4096 == me, keys % 4096, -1), axis=1)
    slots = slots.reshape(n // group, 1, group * cap)
    live = jnp.arange(slot_count, dtype=jnp.int32) < tile_counts.reshape(-1)[0]
    live = jnp.broadcast_to(live[:, None], (slot_count, 128)).astype(jnp.bfloat16)
    grid = setconv(
        packed.reshape(n, cap, channels), slots, live,
        setconv_weights.reshape(-1, slot_count), n_lat, n_lon, cap, group,
    )
    out = encode(grid, conv1_weight, conv2_weight, n_lat, n_lon, tile_rows, tile_cols)
    return out.reshape(tile_rows // 4, tile_cols // 4, channels)


def solution(mesh):
    in_specs = (
        P(("lat", "lon"), None),
        P(),
        P(("lat", "lon")),
        P(("lat", "lon")),
        P("lat", "lon"),
        P("lat", "lon", None),
        P(),
        P(),
    )
    out_specs = P("lat", "lon", None)
    return jax.shard_map(body, mesh=mesh, in_specs=in_specs, out_specs=out_specs, check_vma=False)
```

time: 145 us -> 169 us (1.17); the launches traced: 142 us -> 168 us
  Pallas kernels: 0 us -> 110 us
  matrix products: 37 us -> 0 us
  blocking collectives: 0 us -> 32.3 us
  other arithmetic: 24.2 us -> 0.33 us
  waiting for transfers between devices: 22.8 us -> 0 us
  starting transfers between devices: 19.4 us -> 0 us
  local copies, waits for them, and re-layouts: 37.7 us -> 24.8 us
    pallas_call x0 -> x3, Pallas kernels: none -> 110 us  [the longest x1 64.6 us: setconv(): pl.pallas_call(functools.partial(setconv_kernel, n_lat, n_lon, cap, group...]
    dot_general x14 -> x0, matrix products: 37 us -> none  [the longest x1 18 us: body(): numerator = jnp.dot(masked, obs_block, preferred_element_type=jnp.float32)]
    all_gather x0 -> x1, blocking collectives: none -> 32.3 us  [body(): keys = lax.all_gather(tile_ids * 4096 + slot_offsets, ('lat', 'lon'))]
    gather x3 -> x0, local copies, waits for them, and re-layouts: 23.4 us -> none  [the longest x2 13 us: body(): jnp.take(slot_offsets, source_rows, axis=0)]
    unnamed x36 -> x12, local copies, waits for them, and re-layouts: 1.93 us -> 24.2 us
    all_to_all x2 -> x0, waiting for transfers between devices: 20.3 us -> none  [the longest x1 20.3 us: body(): lax.all_to_all(packed.reshape(peer_count, capacity, row_width), ('lat', '...]
    select_n x4 -> x0, other arithmetic: 13.3 us -> none  [the longest x1 9.95 us: body(): jnp.where(live_mask[None, :], weights_flat, jnp.zeros((), jnp.bfloat16))]
    all_to_all x2 -> x0, starting transfers between devices: 12.1 us -> none  [the longest x1 6.25 us: body(): lax.all_to_all(offsets_out.reshape(peer_count, capacity), ('lat', 'lon'),...]
  transfers between devices with their start and end apart: 6 -> 0, of which waited for: 2 -> 0; matrix products, arithmetic and copies ran while one was open for 39% -> 0% of each run, Pallas kernels for 0% -> 0%
where the time goes in v1:
time: 169 us; the launch traced here: 168 us
  Pallas kernels  110 us (65%)
  blocking collectives  32.3 us (19%)
  local copies, waits for them, and re-layouts  24.8 us (15%)
    pallas_call x1, Pallas kernels, setconv(): pl.pallas_call(functools.partial(setconv_kernel, n_lat, n_lon, cap, group...  64.6 us
    all_gather x1, blocking collectives, body(): keys = lax.all_gather(tile_ids * 4096 + slot_offsets, ('lat', 'lon'))  32.3 us
    pallas_call x1, Pallas kernels, encode(): pl.pallas_call(functools.partial(encode_kernel, n_lat, n_lon, height, wid...  32.2 us
    unnamed x12, local copies, waits for them, and re-layouts  24.2 us
    pallas_call x1, Pallas kernels, project_pack(): pl.pallas_call(functools.partial(project_pack_kernel, steps, rows), grid=...  13.1 us

profile of v1, /device:TPU:17, one launch (start us, length us, event | category | flops | bytes accessed | tf_op | source)
XLA Modules:
  0.0 168.1 jit_solution(13396495744505825108)
XLA Ops:
  0.0 0.0 copy-start.3
  0.0 0.0 copy-start.4
  0.0 21.3 %copy.11.rad_ref = bf16[1024,8461]{1,0:T(8,128)(2,1)} copy(bf16[1024,8461]{0,1:T(8,128)(2,1)} %param.8) | data formatting | bytes 34656256 | tf_op args[0]
  21.3 0.0 copy-done.3
  21.3 0.0 copy-done.4
  21.3 0.0 copy-start
  21.3 2.2 %copy-done = bf16[8461,256]{1,0:T(8,128)(2,1)S(1)} copy-done((bf16[8461,256]{1,0:T(8,128)(2,1)S(1)}, bf16[8461,256]{1,0:T(8,128)(2,1)}, u32[]{:S(2)}) %copy-start) | copy-done | bytes 4332056
  23.5 13.1 %project_pack.1 = bf16[3584,256]{1,0:T(8,128)(2,1)S(1)} custom-call(bf16[1024,8461]{1,0:T(8,128)(2,1)} %copy.11.rad_ref, bf16[8461,256]{1,0:T(8,128)(2,1)S(1)} %copy-done, s32[1,1024]{1,0:T(1,128)S(1)} %bitcast.8), custom_call_target="tpu_custom_call" | custom-call | flops 4436000768 | bytes 23495168 | tf_op jit(solution)/shard_map/project_pack/pallas_call | solution.py:41
  36.6 32.3 %all-gather = s32[32768]{0:T(1024)S(1)} all-gather(s32[1024]{0:T(1024)S(1)} %get-tuple-element.5), channel_id=2, replica_groups=mesh['lat'=4,'lon'=8] {'lat','lon'}, dimensions={0}, use_global_device_ids=true | all-gather | bytes 135168 | tf_op jit(solution)/shard_map/all_gather | solution.py:358
  68.9 0.2 reshape.24
  69.1 0.3 fusion.2
  69.4 0.1 reshape.25.slots_ref
  70.2 0.4 broadcast_in_dim.4.live_ref
  70.6 0.0 copy-start.1
  70.6 0.0 copy-start.2
  70.6 64.6 %setconv.1.grid_ref = bf16[2048,256]{1,0:T(8,128)(2,1)S(1)} custom-call(bf16[32,112,256]{2,1,0:T(8,128)(2,1)S(1)} %bitcast.6, s32[16,1,224]{2,1,0:T(1,128)S(1)} %reshape.25.slots_ref, bf16[2560,128]{1,0:T(8,128)(2,1)S(1)} %broadcast_in_dim.4.live_ref, bf16[2048,2560]{1,0:T(8,128)(2,1)} %bitcast.9), custom_call_target="tpu_custom_call" | custom-call | flops 5368709120 | bytes 10485760 | tf_op jit(solution)/shard_map/setconv/pallas_call | solution.py:173
  135.2 0.0 copy-done.1
  135.2 0.0 copy-done.2
  135.3 32.2 %encode.1 = bf16[128,256]{1,0:T(8,128)(2,1)S(1)} custom-call(bf16[2048,256]{1,0:T(8,128)(2,1)S(1)} %setconv.1.grid_ref, bf16[3,3,256,256]{3,2,1,0:T(8,128)(2,1)S(1)} %copy-done.1, bf16[3,3,256,256]{3,2,1,0:T(8,128)(2,1)S(1)} %copy-done.2), custom_call_target="tpu_custom_call" | custom-call | tf_op jit(solution)/shard_map/encode/pallas_call | solution.py:328
  167.5 0.6 copy.14
  (4 shorter events, 0.1 us)
Async XLA Ops:
  0.0 21.3 %copy-start.3 = (s32[1024]{0:T(1024)S(1)}, s32[1024]{0:T(1024)}, u32[]{:S(2)}) copy-start(s32[1024]{0:T(1024)} %param.11) | copy-start | bytes 12292
  0.0 21.3 %copy-start.4 = (s32[1024]{0:T(1024)S(1)}, s32[1024]{0:T(1024)}, u32[]{:S(2)}) copy-start(s32[1024]{0:T(1024)} %param.10) | copy-start | bytes 12292
  21.3 2.2 %copy-start = (bf16[8461,256]{1,0:T(8,128)(2,1)S(1)}, bf16[8461,256]{1,0:T(8,128)(2,1)}, u32[]{:S(2)}) copy-start(bf16[8461,256]{1,0:T(8,128)(2,1)} %weight_ref.1) | copy-start | bytes 12996100
  70.6 64.7 %copy-start.1 = (bf16[3,3,256,256]{3,2,1,0:T(8,128)(2,1)S(1)}, bf16[3,3,256,256]{3,2,1,0:T(8,128)(2,1)}, u32[]{:S(2)}) copy-start(bf16[3,3,256,256]{3,2,1,0:T(8,128)(2,1)} %k1_ref.1) | copy-start | bytes 3538948
  70.6 64.7 %copy-start.2 = (bf16[3,3,256,256]{3,2,1,0:T(8,128)(2,1)S(1)}, bf16[3,3,256,256]{3,2,1,0:T(8,128)(2,1)}, u32[]{:S(2)}) copy-start(bf16[3,3,256,256]{3,2,1,0:T(8,128)(2,1)} %k2_ref.1) | copy-start | bytes 3538948

commit v2 on v1

--- a/solution.py
+++ b/solution.py
@@ -11,14 +11,26 @@
 MIB = 1024 * 1024
 
 
-def project_pack_kernel(steps, rows, rad_ref, weight_ref, pos_ref, packed_ref, feat_ref):
+def project_pack_kernel(steps, tail, rad_ref, weight_ref, pos_ref, packed_ref, acc_ref, feat_ref):
     step = pl.program_id(0)
-    feat_ref[pl.ds(pl.multiple_of(step * rows, rows), rows), :] = jnp.dot(
-        rad_ref[...], weight_ref[...], preferred_element_type=jnp.float32
-    ).astype(jnp.bfloat16)
+
+    def part(weight, rows):
+        return lax.dot_general(
+            weight, rows, (((0,), (0,)), ((), ())), preferred_element_type=jnp.float32
+        )
+
+    @pl.when(step == 0)
+    def _():
+        acc_ref[...] = part(weight_ref[...], rad_ref[...])
+
+    @pl.when((step > 0) & (step < steps - 1))
+    def _():
+        acc_ref[...] += part(weight_ref[...], rad_ref[...])
 
     @pl.when(step == steps - 1)
     def _():
+        last = acc_ref[...] + part(weight_ref[:tail], rad_ref[:tail])
+        feat_ref[...] = last.T.astype(jnp.bfloat16)
         total = packed_ref.shape[0]
         chunk = 256 if total % 256 == 0 else 128
         obs = feat_ref.shape[0]
@@ -34,21 +46,24 @@
 
 
 def project_pack(radiances, weight, pos, total):
-    obs, raw = radiances.shape
+    raw, obs = radiances.shape
     channels = weight.shape[1]
-    rows = 256
-    steps = obs // rows
+    block = 1024
+    steps = -(-raw // block)
     return pl.pallas_call(
-        functools.partial(project_pack_kernel, steps, rows),
+        functools.partial(project_pack_kernel, steps, raw - (steps - 1) * block),
         grid=(steps,),
         out_shape=jax.ShapeDtypeStruct((total, channels), jnp.bfloat16),
         in_specs=[
-            pl.BlockSpec((rows, raw), lambda i: (i, 0)),
-            pl.BlockSpec((raw, channels), lambda i: (0, 0)),
+            pl.BlockSpec((block, obs), lambda i: (i, 0)),
+            pl.BlockSpec((block, channels), lambda i: (i, 0)),
             pl.BlockSpec((1, obs), lambda i: (0, 0)),
         ],
         out_specs=pl.BlockSpec((total, channels), lambda i: (0, 0)),
-        scratch_shapes=[pltpu.VMEM((obs, channels), jnp.bfloat16)],
+        scratch_shapes=[
+            pltpu.VMEM((channels, obs), jnp.float32),
+            pltpu.VMEM((obs, channels), jnp.bfloat16),
+        ],
         compiler_params=pltpu.CompilerParams(vmem_limit_bytes=48 * MIB),
         cost_estimate=pl.CostEstimate(
             flops=2 * obs * raw * channels,
@@ -59,13 +74,25 @@
     )(radiances, weight, pos)
 
 
+def flipped(value, by, count):
+    result = 0
+    bit = 1
+    while bit < count:
+        result = result + lax.rem(value // bit + by // bit, 2) * bit
+        bit *= 2
+    return result
+
+
 def setconv_kernel(
-    n_lat, n_lon, cap, group, chunk,
+    n_lat, n_lon, cap, chunk,
     packed_ref, slots_ref, live_ref, w_hbm, out_ref,
-    arrived, w_vmem, obs, dens, send_sem, recv_sem, own_sem, w_sem,
+    arrived, slots_in, w_vmem, obs, dens,
+    send_sem, recv_sem, slot_send_sem, slot_recv_sem, own_sem, w_sem,
 ):
     n = n_lat * n_lon
-    me = lax.axis_index("lat") * n_lon + lax.axis_index("lon")
+    lat = lax.axis_index("lat")
+    lon = lax.axis_index("lon")
+    me = lat * n_lon + lon
     cells, slot_count = w_vmem.shape
     chunks = cells // chunk
 
@@ -73,43 +100,58 @@
         part = pl.ds(pl.multiple_of(c * chunk, chunk), chunk)
         return pltpu.make_async_copy(w_hbm.at[part], w_vmem.at[part], w_sem.at[c])
 
-    def send(d):
-        peer = lax.rem(me + d, n)
+    def partner(j):
+        d = lax.rem(11 * j, n)
+        return flipped(lat, d // n_lon, n_lat), flipped(lon, lax.rem(d, n_lon), n_lon)
+
+    def number(j):
+        peer_lat, peer_lon = partner(j)
+        return peer_lat * n_lon + peer_lon
+
+    def row_copy(j, slot):
         return pltpu.make_async_remote_copy(
-            src_ref=packed_ref.at[peer],
-            dst_ref=arrived.at[me],
-            send_sem=send_sem.at[d],
-            recv_sem=recv_sem.at[me],
-            device_id=(peer // n_lon, lax.rem(peer, n_lon)),
+            src_ref=packed_ref.at[number(j)],
+            dst_ref=arrived.at[slot, pl.ds(0, cap)],
+            send_sem=send_sem.at[j],
+            recv_sem=recv_sem.at[slot],
+            device_id=partner(j),
             device_id_type=MESH,
         )
 
-    def arrival(source):
+    def slot_copy(j, slot):
         return pltpu.make_async_remote_copy(
-            src_ref=packed_ref.at[source],
-            dst_ref=arrived.at[source],
-            send_sem=send_sem.at[0],
-            recv_sem=recv_sem.at[source],
-            device_id=(source // n_lon, lax.rem(source, n_lon)),
+            src_ref=slots_ref.at[number(j)],
+            dst_ref=slots_in.at[slot],
+            send_sem=slot_send_sem.at[j],
+            recv_sem=slot_recv_sem.at[slot],
+            device_id=partner(j),
             device_id_type=MESH,
         )
 
     barrier = pltpu.get_barrier_semaphore()
 
     @pl.loop(1, n)
-    def _(d):
-        peer = lax.rem(me + d, n)
-        pl.semaphore_signal(
-            barrier, inc=1, device_id=(peer // n_lon, lax.rem(peer, n_lon)), device_id_type=MESH
-        )
-
-    own = pltpu.make_async_copy(packed_ref.at[me], arrived.at[me], own_sem)
-    own.start()
+    def _(j):
+        pl.semaphore_signal(barrier, inc=1, device_id=partner(j), device_id_type=MESH)
+
+    own_rows = pltpu.make_async_copy(
+        packed_ref.at[me], arrived.at[me, pl.ds(0, cap)], own_sem.at[0]
+    )
+    own_slots = pltpu.make_async_copy(slots_ref.at[me], slots_in.at[me], own_sem.at[1])
+    own_rows.start()
+    own_slots.start()
+    padding = arrived.shape[1] - cap
+    if padding:
+        arrived[:, cap:, :] = jnp.zeros((n, padding, arrived.shape[2]), jnp.bfloat16)
     pl.semaphore_wait(barrier, n - 1)
 
     @pl.loop(1, n)
-    def _(d):
-        send(d).start()
+    def _(j):
+        row_copy(j, me).start()
+
+    @pl.loop(1, n)
+    def _(j):
+        slot_copy(j, me).start()
 
     @pl.loop(0, chunks)
     def _(c):
@@ -125,28 +167,28 @@
             w_vmem[part, :], live_ref[...], preferred_element_type=jnp.float32
         )
 
-    own.wait()
-    width = group * cap
-    groups = n // group
+    own_rows.wait()
+    own_slots.wait()
     obs_chunk = 256
 
-    @pl.loop(0, groups)
+    @pl.loop(0, n // 2)
     def _(k):
-        g = lax.rem(me // group + k, groups)
-        for j in range(group):
-            source = g * group + j
-
-            @pl.when(source != me)
-            def _():
-                arrival(source).wait_recv()
-
-        rows = arrived[pl.ds(g * group, group)].reshape(width, arrived.shape[2])
-        slots = slots_ref[g]
+        sources = [number(2 * k), number(2 * k + 1)]
+
+        @pl.when(k > 0)
+        def _():
+            slot_copy(2 * k, sources[0]).wait_recv()
+            row_copy(2 * k, sources[0]).wait_recv()
+
+        slot_copy(2 * k + 1, sources[1]).wait_recv()
+        row_copy(2 * k + 1, sources[1]).wait_recv()
+        rows = jnp.concatenate([arrived[source] for source in sources], axis=0)
+        slots = jnp.concatenate([slots_in[source] for source in sources], axis=1)
 
         @pl.loop(0, slot_count // obs_chunk)
         def _(c):
             base = pl.multiple_of(c * obs_chunk, obs_chunk)
-            at = lax.broadcasted_iota(jnp.int32, (obs_chunk, width), 0) + base
+            at = lax.broadcasted_iota(jnp.int32, (obs_chunk, slots.shape[1]), 0) + base
             onehot = (at == slots).astype(jnp.float32).astype(jnp.bfloat16)
             placed = jnp.dot(onehot, rows, preferred_element_type=jnp.float32)
             obs[pl.ds(base, obs_chunk), :] += placed.astype(jnp.bfloat16)
@@ -160,29 +202,33 @@
         out_ref[part, :] = (numerator / root).astype(jnp.bfloat16)
 
     @pl.loop(1, n)
-    def _(d):
-        send(d).wait_send()
-
-
-def setconv(packed, slots, live, weights, n_lat, n_lon, cap, group):
-    n = n_lat * n_lon
-    channels = packed.shape[2]
+    def _(j):
+        row_copy(j, me).wait_send()
+        slot_copy(j, me).wait_send()
+
+
+def setconv(packed, slots, live, weights, n_lat, n_lon):
+    n, cap, channels = packed.shape
+    lanes = slots.shape[2]
     cells, slot_count = weights.shape
     chunk = 256
     vmem = pl.BlockSpec(memory_space=pltpu.VMEM)
     return pl.pallas_call(
-        functools.partial(setconv_kernel, n_lat, n_lon, cap, group, chunk),
+        functools.partial(setconv_kernel, n_lat, n_lon, cap, chunk),
         out_shape=jax.ShapeDtypeStruct((cells, channels), jnp.bfloat16),
         in_specs=[vmem, vmem, vmem, pl.BlockSpec(memory_space=pl.ANY)],
         out_specs=vmem,
         scratch_shapes=[
-            pltpu.VMEM((n, cap, channels), jnp.bfloat16),
+            pltpu.VMEM((n, lanes, channels), jnp.bfloat16),
+            pltpu.VMEM((n, 1, lanes), jnp.int32),
             pltpu.VMEM((cells, slot_count), jnp.bfloat16),
             pltpu.VMEM((slot_count, channels), jnp.bfloat16),
             pltpu.VMEM((cells, 128), jnp.float32),
             pltpu.SemaphoreType.DMA((n,)),
             pltpu.SemaphoreType.DMA((n,)),
-            pltpu.SemaphoreType.DMA,
+            pltpu.SemaphoreType.DMA((n,)),
+            pltpu.SemaphoreType.DMA((n,)),
+            pltpu.SemaphoreType.DMA((2,)),
             pltpu.SemaphoreType.DMA((cells // chunk,)),
         ],
         compiler_params=pltpu.CompilerParams(
@@ -349,26 +395,27 @@
     obs_count = radiances.shape[0]
     limit = 7 * (obs_count // n) // 2
     cap = -(-limit // 16) * 16
-    group = max(1, 256 // cap)
     tile_rows, tile_cols, slot_count = setconv_weights.shape
     channels = project_weight.shape[1]
 
     place = jnp.arange(obs_count, dtype=jnp.int32) % cap
     pos = (tile_ids * cap + place).reshape(1, obs_count)
-    keys = lax.all_gather(tile_ids * 4096 + slot_offsets, ("lat", "lon"))
-    packed = project_pack(radiances, project_weight, pos, n * cap)
-
-    me = lax.axis_index("lat") * n_lon + lax.axis_index("lon")
+    packed = project_pack(radiances.T, project_weight, pos, n * cap)
+
+    lanes = -(-cap // 128) * 128
     turns = -(-obs_count // cap)
-    keys = jnp.pad(keys, ((0, 0), (0, turns * cap - obs_count)), constant_values=-1)
-    keys = keys.reshape(n, turns, cap)
-    slots = jnp.max(jnp.where(keys // 4096 == me, keys % 4096, -1), axis=1)
-    slots = slots.reshape(n // group, 1, group * cap)
+    spare = (0, turns * cap - obs_count)
+    tiles = jnp.pad(tile_ids, spare, constant_values=-1).reshape(1, turns, cap)
+    offsets = jnp.pad(slot_offsets, spare).reshape(1, turns, cap)
+    target = jnp.arange(n, dtype=jnp.int32)[:, None, None]
+    slots = jnp.max(jnp.where(tiles == target, offsets, -1), axis=1)
+    slots = jnp.pad(slots, ((0, 0), (0, lanes - cap)), constant_values=-1)
+    slots = slots.reshape(n, 1, lanes)
     live = jnp.arange(slot_count, dtype=jnp.int32) < tile_counts.reshape(-1)[0]
     live = jnp.broadcast_to(live[:, None], (slot_count, 128)).astype(jnp.bfloat16)
     grid = setconv(
         packed.reshape(n, cap, channels), slots, live,
-        setconv_weights.reshape(-1, slot_count), n_lat, n_lon, cap, group,
+        setconv_weights.reshape(-1, slot_count), n_lat, n_lon,
     )
     out = encode(grid, conv1_weight, conv2_weight, n_lat, n_lon, tile_rows, tile_cols)
     return out.reshape(tile_rows // 4, tile_cols // 4, channels)

time: 169 us -> 115 us (0.68)
  blocking collectives: 32.3 us -> 0 us
  local copies, waits for them, and re-layouts: 24.8 us -> 4.81 us
  Pallas kernels: 110 us -> 108 us
    all_gather x1 -> x0, blocking collectives: 32.3 us -> none  [body(): keys = lax.all_gather(tile_ids * 4096 + slot_offsets, ('lat', 'lon'))]
    unnamed x12 -> x7, local copies, waits for them, and re-layouts: 24.2 us -> 2.87 us
    pallas_call x1, Pallas kernels: 32.2 us -> 18 us  [encode(): pl.pallas_call(functools.partial(encode_kernel, n_lat, n_lon, height, wid...]
    pallas_call x2, Pallas kernels: 77.7 us -> 90.4 us  [the longest x1 74.9 us: setconv(): pl.pallas_call(functools.partial(setconv_kernel, n_lat, n_lon, cap, chunk...]
where the time goes in v2:
time: 115 us
  Pallas kernels  108 us (94%)
  local copies, waits for them, and re-layouts  4.81 us (4%)
    pallas_call x1, Pallas kernels, setconv(): pl.pallas_call(functools.partial(setconv_kernel, n_lat, n_lon, cap, chunk...  74.9 us
    pallas_call x1, Pallas kernels, encode(): pl.pallas_call(functools.partial(encode_kernel, n_lat, n_lon, height, wid...  18 us
    pallas_call x1, Pallas kernels, project_pack(): pl.pallas_call(functools.partial(project_pack_kernel, steps, raw - (steps...  15.5 us
    unnamed x7, local copies, waits for them, and re-layouts  2.87 us

profile of v2, /device:TPU:17, one launch (start us, length us, event | category | flops | bytes accessed | tf_op | source)
XLA Modules:
  0.0 114.8 jit_solution(14541034028415515789)
XLA Ops:
  0.7 0.7 fusion.1
  1.4 0.7 pad.12
  2.0 0.1 broadcast_in_dim.21
  2.1 0.7 pad.11
  2.8 0.1 eq.17
  3.0 0.4 broadcast_in_dim.24.live_ref
  3.4 0.0 copy-start
  3.4 2.2 %copy-done = bf16[8461,256]{1,0:T(8,128)(2,1)S(1)} copy-done((bf16[8461,256]{1,0:T(8,128)(2,1)S(1)}, bf16[8461,256]{1,0:T(8,128)(2,1)}, u32[]{:S(2)}) %copy-start) | copy-done | bytes 4332056
  5.6 15.5 %project_pack.1 = bf16[3584,256]{1,0:T(8,128)(2,1)S(1)} custom-call(bf16[8461,1024]{1,0:T(8,128)(2,1)} %bitcast.12, bf16[8461,256]{1,0:T(8,128)(2,1)S(1)} %copy-done, s32[1,1024]{1,0:T(1,128)S(1)} %bitcast.10), custom_call_target="tpu_custom_call" | custom-call | flops 4436000768 | bytes 23495168 | tf_op jit(solution)/shard_map/project_pack/pallas_call | solution.py:53
  21.1 0.0 copy-start.1
  21.1 0.0 copy-start.2
  21.1 74.9 %setconv.1.grid_ref = bf16[2048,256]{1,0:T(8,128)(2,1)S(1)} custom-call(bf16[32,112,256]{2,1,0:T(8,128)(2,1)S(1)} %bitcast.8, s32[32,1,128]{2,1,0:T(1,128)S(1)} %bitcast.11, bf16[2560,128]{1,0:T(8,128)(2,1)S(1)} %broadcast_in_dim.24.live_ref, bf16[2048,2560]{1,0:T(8,128)(2,1)} %bitcast.13), custom_call_target="tpu_custom_call" | custom-call | flops 5368709120 | bytes 10485760 | tf_op jit(solution)/shard_map/setconv/pallas_call | solution.py:216
  96.1 0.0 copy-done.1
  96.1 0.0 copy-done.2
  96.1 18.0 %encode.1 = bf16[128,256]{1,0:T(8,128)(2,1)S(1)} custom-call(bf16[2048,256]{1,0:T(8,128)(2,1)S(1)} %setconv.1.grid_ref, bf16[3,3,256,256]{3,2,1,0:T(8,128)(2,1)S(1)} %copy-done.1, bf16[3,3,256,256]{3,2,1,0:T(8,128)(2,1)S(1)} %copy-done.2), custom_call_target="tpu_custom_call" | custom-call | tf_op jit(solution)/shard_map/encode/pallas_call | solution.py:374
  114.1 0.6 copy.11
  (3 shorter events, 0.0 us)
Async XLA Ops:
  3.4 2.2 %copy-start = (bf16[8461,256]{1,0:T(8,128)(2,1)S(1)}, bf16[8461,256]{1,0:T(8,128)(2,1)}, u32[]{:S(2)}) copy-start(bf16[8461,256]{1,0:T(8,128)(2,1)} %weight_ref.1) | copy-start | bytes 12996100
  21.1 75.0 %copy-start.1 = (bf16[3,3,256,256]{3,2,1,0:T(8,128)(2,1)S(1)}, bf16[3,3,256,256]{3,2,1,0:T(8,128)(2,1)}, u32[]{:S(2)}) copy-start(bf16[3,3,256,256]{3,2,1,0:T(8,128)(2,1)} %k1_ref.1) | copy-start | bytes 3538948
  21.1 75.0 %copy-start.2 = (bf16[3,3,256,256]{3,2,1,0:T(8,128)(2,1)S(1)}, bf16[3,3,256,256]{3,2,1,0:T(8,128)(2,1)}, u32[]{:S(2)}) copy-start(bf16[3,3,256,256]{3,2,1,0:T(8,128)(2,1)} %k2_ref.1) | copy-start | bytes 3538948

commit v3 on v2

--- a/solution.py
+++ b/solution.py
@@ -74,25 +74,33 @@
     )(radiances, weight, pos)
 
 
-def flipped(value, by, count):
-    result = 0
-    bit = 1
-    while bit < count:
-        result = result + lax.rem(value // bit + by // bit, 2) * bit
-        bit *= 2
-    return result
-
-
-def setconv_kernel(
-    n_lat, n_lon, cap, chunk,
-    packed_ref, slots_ref, live_ref, w_hbm, out_ref,
-    arrived, slots_in, w_vmem, obs, dens,
-    send_sem, recv_sem, slot_send_sem, slot_recv_sem, own_sem, w_sem,
-):
-    n = n_lat * n_lon
-    lat = lax.axis_index("lat")
-    lon = lax.axis_index("lon")
-    me = lat * n_lon + lon
+def density_kernel(w_ref, live_ref, dens_ref):
+    dens_ref[...] = jnp.dot(w_ref[...], live_ref[...], preferred_element_type=jnp.float32)
+
+
+def density(weights, live):
+    cells, slot_count = weights.shape
+    chunk = 256
+    return pl.pallas_call(
+        density_kernel,
+        grid=(cells // chunk,),
+        out_shape=jax.ShapeDtypeStruct((cells, 128), jnp.float32),
+        in_specs=[
+            pl.BlockSpec((chunk, slot_count), lambda i: (i, 0)),
+            pl.BlockSpec((slot_count, 128), lambda i: (0, 0)),
+        ],
+        out_specs=pl.BlockSpec((chunk, 128), lambda i: (i, 0)),
+        compiler_params=pltpu.CompilerParams(vmem_limit_bytes=16 * MIB),
+        cost_estimate=pl.CostEstimate(
+            flops=2 * cells * slot_count * 128,
+            bytes_accessed=2 * cells * slot_count,
+            transcendentals=0,
+        ),
+        name="density",
+    )(weights, live)
+
+
+def setconv_kernel(chunk, rows_ref, slots_ref, dens_ref, w_hbm, out_ref, w_vmem, obs, w_sem):
     cells, slot_count = w_vmem.shape
     chunks = cells // chunk
 
@@ -100,147 +108,54 @@
         part = pl.ds(pl.multiple_of(c * chunk, chunk), chunk)
         return pltpu.make_async_copy(w_hbm.at[part], w_vmem.at[part], w_sem.at[c])
 
-    def partner(j):
-        d = lax.rem(11 * j, n)
-        return flipped(lat, d // n_lon, n_lat), flipped(lon, lax.rem(d, n_lon), n_lon)
-
-    def number(j):
-        peer_lat, peer_lon = partner(j)
-        return peer_lat * n_lon + peer_lon
-
-    def row_copy(j, slot):
-        return pltpu.make_async_remote_copy(
-            src_ref=packed_ref.at[number(j)],
-            dst_ref=arrived.at[slot, pl.ds(0, cap)],
-            send_sem=send_sem.at[j],
-            recv_sem=recv_sem.at[slot],
-            device_id=partner(j),
-            device_id_type=MESH,
-        )
-
-    def slot_copy(j, slot):
-        return pltpu.make_async_remote_copy(
-            src_ref=slots_ref.at[number(j)],
-            dst_ref=slots_in.at[slot],
-            send_sem=slot_send_sem.at[j],
-            recv_sem=slot_recv_sem.at[slot],
-            device_id=partner(j),
-            device_id_type=MESH,
-        )
-
-    barrier = pltpu.get_barrier_semaphore()
-
-    @pl.loop(1, n)
-    def _(j):
-        pl.semaphore_signal(barrier, inc=1, device_id=partner(j), device_id_type=MESH)
-
-    own_rows = pltpu.make_async_copy(
-        packed_ref.at[me], arrived.at[me, pl.ds(0, cap)], own_sem.at[0]
-    )
-    own_slots = pltpu.make_async_copy(slots_ref.at[me], slots_in.at[me], own_sem.at[1])
-    own_rows.start()
-    own_slots.start()
-    padding = arrived.shape[1] - cap
-    if padding:
-        arrived[:, cap:, :] = jnp.zeros((n, padding, arrived.shape[2]), jnp.bfloat16)
-    pl.semaphore_wait(barrier, n - 1)
-
-    @pl.loop(1, n)
-    def _(j):
-        row_copy(j, me).start()
-
-    @pl.loop(1, n)
-    def _(j):
-        slot_copy(j, me).start()
-
     @pl.loop(0, chunks)
     def _(c):
         w_copy(c).start()
 
-    obs[...] = jnp.zeros_like(obs)
+    width = slots_ref.shape[1]
+    part_slots = 128
+
+    @pl.loop(0, slot_count // part_slots)
+    def _(c):
+        base = pl.multiple_of(c * part_slots, part_slots)
+        at = lax.broadcasted_iota(jnp.int32, (part_slots, width), 0) + base
+        onehot = (at == slots_ref[...]).astype(jnp.float32).astype(jnp.bfloat16)
+        placed = jnp.dot(onehot, rows_ref[...], preferred_element_type=jnp.float32)
+        obs[pl.ds(base, part_slots), :] = placed.astype(jnp.bfloat16)
 
     @pl.loop(0, chunks)
     def _(c):
         w_copy(c).wait()
         part = pl.ds(pl.multiple_of(c * chunk, chunk), chunk)
-        dens[part, :] = jnp.dot(
-            w_vmem[part, :], live_ref[...], preferred_element_type=jnp.float32
-        )
-
-    own_rows.wait()
-    own_slots.wait()
-    obs_chunk = 256
-
-    @pl.loop(0, n // 2)
-    def _(k):
-        sources = [number(2 * k), number(2 * k + 1)]
-
-        @pl.when(k > 0)
-        def _():
-            slot_copy(2 * k, sources[0]).wait_recv()
-            row_copy(2 * k, sources[0]).wait_recv()
-
-        slot_copy(2 * k + 1, sources[1]).wait_recv()
-        row_copy(2 * k + 1, sources[1]).wait_recv()
-        rows = jnp.concatenate([arrived[source] for source in sources], axis=0)
-        slots = jnp.concatenate([slots_in[source] for source in sources], axis=1)
-
-        @pl.loop(0, slot_count // obs_chunk)
-        def _(c):
-            base = pl.multiple_of(c * obs_chunk, obs_chunk)
-            at = lax.broadcasted_iota(jnp.int32, (obs_chunk, slots.shape[1]), 0) + base
-            onehot = (at == slots).astype(jnp.float32).astype(jnp.bfloat16)
-            placed = jnp.dot(onehot, rows, preferred_element_type=jnp.float32)
-            obs[pl.ds(base, obs_chunk), :] += placed.astype(jnp.bfloat16)
-
-    @pl.loop(0, chunks)
-    def _(c):
-        part = pl.ds(pl.multiple_of(c * chunk, chunk), chunk)
         numerator = jnp.dot(w_vmem[part, :], obs[...], preferred_element_type=jnp.float32)
-        root = jnp.sqrt(dens[part, :])
+        root = jnp.sqrt(dens_ref[part, :])
         root = jnp.concatenate([root] * (numerator.shape[1] // root.shape[1]), axis=1)
         out_ref[part, :] = (numerator / root).astype(jnp.bfloat16)
 
-    @pl.loop(1, n)
-    def _(j):
-        row_copy(j, me).wait_send()
-        slot_copy(j, me).wait_send()
-
-
-def setconv(packed, slots, live, weights, n_lat, n_lon):
-    n, cap, channels = packed.shape
-    lanes = slots.shape[2]
+
+def setconv(rows, slots, dens, weights):
+    channels = rows.shape[1]
     cells, slot_count = weights.shape
     chunk = 256
     vmem = pl.BlockSpec(memory_space=pltpu.VMEM)
     return pl.pallas_call(
-        functools.partial(setconv_kernel, n_lat, n_lon, cap, chunk),
+        functools.partial(setconv_kernel, chunk),
         out_shape=jax.ShapeDtypeStruct((cells, channels), jnp.bfloat16),
         in_specs=[vmem, vmem, vmem, pl.BlockSpec(memory_space=pl.ANY)],
         out_specs=vmem,
         scratch_shapes=[
-            pltpu.VMEM((n, lanes, channels), jnp.bfloat16),
-            pltpu.VMEM((n, 1, lanes), jnp.int32),
             pltpu.VMEM((cells, slot_count), jnp.bfloat16),
             pltpu.VMEM((slot_count, channels), jnp.bfloat16),
-            pltpu.VMEM((cells, 128), jnp.float32),
-            pltpu.SemaphoreType.DMA((n,)),
-            pltpu.SemaphoreType.DMA((n,)),
-            pltpu.SemaphoreType.DMA((n,)),
-            pltpu.SemaphoreType.DMA((n,)),
-            pltpu.SemaphoreType.DMA((2,)),
             pltpu.SemaphoreType.DMA((cells // chunk,)),
         ],
-        compiler_params=pltpu.CompilerParams(
-            collective_id=0, has_side_effects=True, vmem_limit_bytes=48 * MIB
-        ),
+        compiler_params=pltpu.CompilerParams(vmem_limit_bytes=48 * MIB),
         cost_estimate=pl.CostEstimate(
             flops=4 * cells * slot_count * channels,
             bytes_accessed=2 * cells * slot_count,
             transcendentals=0,
         ),
         name="setconv",
-    )(packed, slots, live, weights)
+    )(rows, slots, dens, weights)
 
 
 def load_rows(ref, rows):
@@ -379,7 +294,7 @@
         scratch_shapes=scratch(height, width) + scratch(height // 2, width // 2)
         + [pltpu.SemaphoreType.DMA((2, 8))],
         compiler_params=pltpu.CompilerParams(
-            collective_id=1, has_side_effects=True, vmem_limit_bytes=48 * MIB
+            collective_id=0, has_side_effects=True, vmem_limit_bytes=48 * MIB
         ),
         name="encode",
     )(grid, kernel1, kernel2)
@@ -400,23 +315,22 @@
 
     place = jnp.arange(obs_count, dtype=jnp.int32) % cap
     pos = (tile_ids * cap + place).reshape(1, obs_count)
-    packed = project_pack(radiances.T, project_weight, pos, n * cap)
-
-    lanes = -(-cap // 128) * 128
     turns = -(-obs_count // cap)
     spare = (0, turns * cap - obs_count)
     tiles = jnp.pad(tile_ids, spare, constant_values=-1).reshape(1, turns, cap)
     offsets = jnp.pad(slot_offsets, spare).reshape(1, turns, cap)
     target = jnp.arange(n, dtype=jnp.int32)[:, None, None]
     slots = jnp.max(jnp.where(tiles == target, offsets, -1), axis=1)
-    slots = jnp.pad(slots, ((0, 0), (0, lanes - cap)), constant_values=-1)
-    slots = slots.reshape(n, 1, lanes)
+    slots = lax.all_to_all(slots, ("lat", "lon"), 0, 0, tiled=True).reshape(1, n * cap)
+
+    packed = project_pack(radiances.T, project_weight, pos, n * cap)
+    rows = lax.all_to_all(
+        packed.reshape(n, cap, channels), ("lat", "lon"), 0, 0, tiled=True
+    ).reshape(n * cap, channels)
     live = jnp.arange(slot_count, dtype=jnp.int32) < tile_counts.reshape(-1)[0]
     live = jnp.broadcast_to(live[:, None], (slot_count, 128)).astype(jnp.bfloat16)
-    grid = setconv(
-        packed.reshape(n, cap, channels), slots, live,
-        setconv_weights.reshape(-1, slot_count), n_lat, n_lon,
-    )
+    weights = setconv_weights.reshape(-1, slot_count)
+    grid = setconv(rows, slots, density(weights, live), weights)
     out = encode(grid, conv1_weight, conv2_weight, n_lat, n_lon, tile_rows, tile_cols)
     return out.reshape(tile_rows // 4, tile_cols // 4, channels)
 

time: 115 us -> 100 us (0.87)
  Pallas kernels: 108 us -> 44.2 us
  waiting for transfers between devices: 0 us -> 31.5 us
  starting transfers between devices: 0 us -> 12.1 us
  local copies, waits for them, and re-layouts: 4.81 us -> 9.38 us
  other arithmetic: 0.74 us -> 2.03 us
    pallas_call x1 -> x2, Pallas kernels: 74.9 us -> 16.4 us  [the longest x1 12.4 us: setconv(): pl.pallas_call(functools.partial(setconv_kernel, chunk), out_shape=jax.Sh...]
    all_to_all x0 -> x2, waiting for transfers between devices: none -> 31.5 us  [the longest x1 31.5 us: body(): lax.all_to_all(packed.reshape(n, cap, channels), ('lat', 'lon'), 0, 0, ti...]
    all_to_all x0 -> x2, starting transfers between devices: none -> 12.1 us  [the longest x1 6.25 us: body(): lax.all_to_all(slots, ('lat', 'lon'), 0, 0, tiled=True).reshape(1, n * cap)]
    pallas_call x1, Pallas kernels: 18 us -> 11.1 us  [encode(): pl.pallas_call(functools.partial(encode_kernel, n_lat, n_lon, height, wid...]
    unnamed x7 -> x9, local copies, waits for them, and re-layouts: 2.87 us -> 6.84 us
    pallas_call x1, Pallas kernels: 15.5 us -> 16.7 us  [project_pack(): pl.pallas_call(functools.partial(project_pack_kernel, steps, raw - (steps...]
  transfers between devices with their start and end apart: 0 -> 2, of which waited for: 0 -> 1; matrix products, arithmetic and copies ran while one was open for 0% -> 2% of each run, Pallas kernels for 0% -> 21%
where the time goes in v3:
time: 100 us; the launch traced here: 99.9 us
  Pallas kernels  44.2 us (44%)
  waiting for transfers between devices  31.5 us (32%)
  starting transfers between devices  12.1 us (12%)
  local copies, waits for them, and re-layouts  9.38 us (9%)
  other arithmetic  2.03 us (2%)
    all_to_all x1, waiting for transfers between devices, body(): lax.all_to_all(packed.reshape(n, cap, channels), ('lat', 'lon'), 0, 0, ti...  31.5 us
    pallas_call x1, Pallas kernels, project_pack(): pl.pallas_call(functools.partial(project_pack_kernel, steps, raw - (steps...  16.7 us
    pallas_call x1, Pallas kernels, setconv(): pl.pallas_call(functools.partial(setconv_kernel, chunk), out_shape=jax.Sh...  12.4 us
    pallas_call x1, Pallas kernels, encode(): pl.pallas_call(functools.partial(encode_kernel, n_lat, n_lon, height, wid...  11.1 us
    unnamed x9, local copies, waits for them, and re-layouts  6.84 us
    all_to_all x1, starting transfers between devices, body(): lax.all_to_all(slots, ('lat', 'lon'), 0, 0, tiled=True).reshape(1, n * cap)  6.25 us
    all_to_all x1, starting transfers between devices, body(): lax.all_to_all(packed.reshape(n, cap, channels), ('lat', 'lon'), 0, 0, ti...  5.83 us
    pallas_call x1, Pallas kernels, density(): pl.pallas_call(density_kernel, grid=(cells // chunk,), out_shape=jax.Shap...  3.95 us
  transfers between devices with their start and end apart: 2, of which 1 were waited for; matrix products, arithmetic and copies ran while one was open for 2% of the time, Pallas kernels for 21%

profile of v3, /device:TPU:17, one launch (start us, length us, event | category | flops | bytes accessed | tf_op | source)
XLA Modules:
  0.0 99.9 jit_solution(7794200538612242379)
XLA Ops:
  0.0 0.7 pad.8
  0.7 0.1 broadcast_in_dim.21
  0.8 0.7 pad.7
  1.5 0.1 eq.17
  1.5 0.6 select_reduce_fusion
  2.2 6.2 %all-to-all-start.1 = ((s32[32,1,112]{2,1,0:T(1,128)}), s32[32,1,112]{2,1,0:T(1,128)S(1)}, u32[]{:S(2)}, u32[]{:S(2)}) async-start(s32[32,1,112]{2,1,0:T(1,128)} %bitcast.5), calls=%async_computation.1 | async-start | bytes 32768 | tf_op jit(solution)/shard_map/all_to_all | solution.py:324
  8.4 0.7 fusion.1
  9.1 0.0 copy-start.1
  9.1 2.2 %copy-done.1 = bf16[8461,256]{1,0:T(8,128)(2,1)S(1)} copy-done((bf16[8461,256]{1,0:T(8,128)(2,1)S(1)}, bf16[8461,256]{1,0:T(8,128)(2,1)}, u32[]{:S(2)}) %copy-start.1) | copy-done | bytes 4332056
  11.4 16.7 %project_pack.1 = bf16[3584,256]{1,0:T(8,128)(2,1)} custom-call(bf16[8461,1024]{1,0:T(8,128)(2,1)} %bitcast.16, bf16[8461,256]{1,0:T(8,128)(2,1)S(1)} %copy-done.1, s32[1,1024]{1,0:T(1,128)S(1)} %bitcast.15), custom_call_target="tpu_custom_call" | custom-call | flops 4436000768 | bytes 23495168 | tf_op jit(solution)/shard_map/project_pack/pallas_call | solution.py:53
  28.1 0.0 all-to-all-done.1
  28.1 5.8 %all-to-all-start = ((bf16[32,112,256]{2,1,0:T(8,128)(2,1)}), bf16[32,112,256]{2,1,0:T(8,128)(2,1)S(1)}, u32[]{:S(2)}, u32[]{:S(2)}) async-start(bf16[32,112,256]{2,1,0:T(8,128)(2,1)} %bitcast.2), calls=%async_computation | async-start | bytes 3670016 | tf_op jit(solution)/shard_map/all_to_all | solution.py:327
  34.6 0.4 broadcast_in_dim.24.live_ref
  35.0 0.0 copy-start
  35.0 4.0 %copy-done = bf16[64,32,2560]{2,1,0:T(8,128)(2,1)S(1)} copy-done((bf16[64,32,2560]{2,1,0:T(8,128)(2,1)S(1)}, bf16[64,32,2560]{2,1,0:T(8,128)(2,1)}, u32[]{:S(2)}) %copy-start) | copy-done | bytes 10485784
  39.0 3.9 %density.1.dens_ref = f32[2048,128]{1,0:T(8,128)S(1)} custom-call(bf16[2048,2560]{1,0:T(8,128)(2,1)S(1)} %bitcast.12, bf16[2560,128]{1,0:T(8,128)(2,1)S(1)} %broadcast_in_dim.24.live_ref), custom_call_target="tpu_custom_call" | custom-call | flops 1342177280 | bytes 10485760 | tf_op jit(solution)/shard_map/density/pallas_call | solution.py:84
  43.0 0.5 broadcast.14
  43.5 0.7 reduce.3
  44.2 0.1 reshape.32.slots_ref
  44.3 31.5 %all-to-all-done = bf16[32,112,256]{2,1,0:T(8,128)(2,1)S(1)} async-done(((bf16[32,112,256]{2,1,0:T(8,128)(2,1)}), bf16[32,112,256]{2,1,0:T(8,128)(2,1)S(1)}, u32[]{:S(2)}, u32[]{:S(2)}) %all-to-all-start) | async-done | bytes 1835040 | tf_op jit(solution)/shard_map/all_to_all | solution.py:327
  75.7 0.0 copy-start.2
  75.7 0.0 copy-start.3
  75.7 12.4 %setconv.1.grid_ref = bf16[2048,256]{1,0:T(8,128)(2,1)S(1)} custom-call(bf16[3584,256]{1,0:T(8,128)(2,1)S(1)} %bitcast.13, s32[1,3584]{1,0:T(1,128)S(1)} %reshape.32.slots_ref, f32[2048,128]{1,0:T(8,128)S(1)} %density.1.dens_ref, bf16[2048,2560]{1,0:T(8,128)(2,1)} %bitcast.11), custom_call_target="tpu_custom_call" | custom-call | flops 5368709120 | bytes 10485760 | tf_op jit(solution)/shard_map/setconv/pallas_call | solution.py:141
  88.2 0.0 copy-done.2
  88.2 0.0 copy-done.3
  88.2 11.1 %encode.1 = bf16[128,256]{1,0:T(8,128)(2,1)S(1)} custom-call(bf16[2048,256]{1,0:T(8,128)(2,1)S(1)} %setconv.1.grid_ref, bf16[3,3,256,256]{3,2,1,0:T(8,128)(2,1)S(1)} %copy-done.2, bf16[3,3,256,256]{3,2,1,0:T(8,128)(2,1)S(1)} %copy-done.3), custom_call_target="tpu_custom_call" | custom-call | tf_op jit(solution)/shard_map/encode/pallas_call | solution.py:289
  99.3 0.6 copy.12
  (1 shorter events, 0.0 us)
Async XLA Ops:
  2.2 25.9 %all-to-all-start.1 = ((s32[32,1,112]{2,1,0:T(1,128)}), s32[32,1,112]{2,1,0:T(1,128)S(1)}, u32[]{:S(2)}, u32[]{:S(2)}) async-start(s32[32,1,112]{2,1,0:T(1,128)} %bitcast.5), calls=%async_computation.1 | async-start | bytes 32768 | tf_op jit(solution)/shard_map/all_to_all | solution.py:324
  9.1 2.2 %copy-start.1 = (bf16[8461,256]{1,0:T(8,128)(2,1)S(1)}, bf16[8461,256]{1,0:T(8,128)(2,1)}, u32[]{:S(2)}) copy-start(bf16[8461,256]{1,0:T(8,128)(2,1)} %weight_ref.1) | copy-start | bytes 12996100
  28.1 47.6 %all-to-all-start = ((bf16[32,112,256]{2,1,0:T(8,128)(2,1)}), bf16[32,112,256]{2,1,0:T(8,128)(2,1)S(1)}, u32[]{:S(2)}, u32[]{:S(2)}) async-start(bf16[32,112,256]{2,1,0:T(8,128)(2,1)} %bitcast.2), calls=%async_computation | async-start | bytes 3670016 | tf_op jit(solution)/shard_map/all_to_all | solution.py:327
  35.0 4.0 %copy-start = (bf16[64,32,2560]{2,1,0:T(8,128)(2,1)S(1)}, bf16[64,32,2560]{2,1,0:T(8,128)(2,1)}, u32[]{:S(2)}) copy-start(bf16[64,32,2560]{2,1,0:T(8,128)(2,1)} %param.13) | copy-start | bytes 31457284
  75.7 12.4 %copy-start.2 = (bf16[3,3,256,256]{3,2,1,0:T(8,128)(2,1)S(1)}, bf16[3,3,256,256]{3,2,1,0:T(8,128)(2,1)}, u32[]{:S(2)}) copy-start(bf16[3,3,256,256]{3,2,1,0:T(8,128)(2,1)} %k1_ref.1) | copy-start | bytes 3538948
  75.7 12.4 %copy-start.3 = (bf16[3,3,256,256]{3,2,1,0:T(8,128)(2,1)S(1)}, bf16[3,3,256,256]{3,2,1,0:T(8,128)(2,1)}, u32[]{:S(2)}) copy-start(bf16[3,3,256,256]{3,2,1,0:T(8,128)(2,1)} %k2_ref.1) | copy-start | bytes 3538948

commit v4 on v3

--- a/solution.py
+++ b/solution.py
@@ -32,7 +32,7 @@
         last = acc_ref[...] + part(weight_ref[:tail], rad_ref[:tail])
         feat_ref[...] = last.T.astype(jnp.bfloat16)
         total = packed_ref.shape[0]
-        chunk = 256 if total % 256 == 0 else 128
+        chunk = 512 if total % 512 == 0 else 128
         obs = feat_ref.shape[0]
 
         @pl.loop(0, total // chunk)
@@ -48,7 +48,7 @@
 def project_pack(radiances, weight, pos, total):
     raw, obs = radiances.shape
     channels = weight.shape[1]
-    block = 1024
+    block = 2048
     steps = -(-raw // block)
     return pl.pallas_call(
         functools.partial(project_pack_kernel, steps, raw - (steps - 1) * block),
@@ -64,7 +64,7 @@
             pltpu.VMEM((channels, obs), jnp.float32),
             pltpu.VMEM((obs, channels), jnp.bfloat16),
         ],
-        compiler_params=pltpu.CompilerParams(vmem_limit_bytes=48 * MIB),
+        compiler_params=pltpu.CompilerParams(vmem_limit_bytes=60 * MIB),
         cost_estimate=pl.CostEstimate(
             flops=2 * obs * raw * channels,
             bytes_accessed=2 * (obs * raw + raw * channels + total * channels),
@@ -113,7 +113,7 @@
         w_copy(c).start()
 
     width = slots_ref.shape[1]
-    part_slots = 128
+    part_slots = 512
 
     @pl.loop(0, slot_count // part_slots)
     def _(c):
@@ -136,7 +136,7 @@
 def setconv(rows, slots, dens, weights):
     channels = rows.shape[1]
     cells, slot_count = weights.shape
-    chunk = 256
+    chunk = 512
     vmem = pl.BlockSpec(memory_space=pltpu.VMEM)
     return pl.pallas_call(
         functools.partial(setconv_kernel, chunk),

time: 100 us -> 92.7 us (0.927)
  Pallas kernels: 44.2 us -> 38.2 us
  local copies, waits for them, and re-layouts: 9.38 us -> 7.15 us
    pallas_call x1, Pallas kernels: 12.4 us -> 9 us  [setconv(): pl.pallas_call(functools.partial(setconv_kernel, chunk), out_shape=jax.Sh...]
    pallas_call x1, Pallas kernels: 16.7 us -> 14.2 us  [project_pack(): pl.pallas_call(functools.partial(project_pack_kernel, steps, raw - (steps...]
    unnamed x9 -> x7, local copies, waits for them, and re-layouts: 6.84 us -> 4.61 us
  transfers between devices with their start and end apart: 2 -> 2, of which waited for: 1 -> 1; matrix products, arithmetic and copies ran while one was open for 2% -> 3% of each run, Pallas kernels for 21% -> 20%
where the time goes in v4:
time: 92.7 us; the launch traced here: 92.3 us
  Pallas kernels  38.2 us (41%)
  waiting for transfers between devices  31.5 us (34%)
  starting transfers between devices  12.1 us (13%)
  local copies, waits for them, and re-layouts  7.15 us (8%)
  other arithmetic  2.62 us (3%)
    all_to_all x1, waiting for transfers between devices, body(): lax.all_to_all(packed.reshape(n, cap, channels), ('lat', 'lon'), 0, 0, ti...  31.5 us
    pallas_call x1, Pallas kernels, project_pack(): pl.pallas_call(functools.partial(project_pack_kernel, steps, raw - (steps...  14.2 us
    pallas_call x1, Pallas kernels, encode(): pl.pallas_call(functools.partial(encode_kernel, n_lat, n_lon, height, wid...  11.1 us
    pallas_call x1, Pallas kernels, setconv(): pl.pallas_call(functools.partial(setconv_kernel, chunk), out_shape=jax.Sh...  9 us
    all_to_all x1, starting transfers between devices, body(): lax.all_to_all(slots, ('lat', 'lon'), 0, 0, tiled=True).reshape(1, n * cap)  6.25 us
    all_to_all x1, starting transfers between devices, body(): lax.all_to_all(packed.reshape(n, cap, channels), ('lat', 'lon'), 0, 0, ti...  5.84 us
    unnamed x7, local copies, waits for them, and re-layouts  4.61 us
    pallas_call x1, Pallas kernels, density(): pl.pallas_call(density_kernel, grid=(cells // chunk,), out_shape=jax.Shap...  3.95 us
  transfers between devices with their start and end apart: 2, of which 1 were waited for; matrix products, arithmetic and copies ran while one was open for 3% of the time, Pallas kernels for 20%

profile of v4, /device:TPU:17, one launch (start us, length us, event | category | flops | bytes accessed | tf_op | source)
XLA Modules:
  0.0 92.3 jit_solution(13082133719210786039)
XLA Ops:
  0.0 0.7 pad.8
  0.7 0.1 broadcast_in_dim.21
  0.8 0.7 pad.7
  1.5 0.1 eq.17
  1.5 0.6 select_reduce_fusion
  2.2 6.2 %all-to-all-start.1 = ((s32[32,1,112]{2,1,0:T(1,128)}), s32[32,1,112]{2,1,0:T(1,128)S(1)}, u32[]{:S(2)}, u32[]{:S(2)}) async-start(s32[32,1,112]{2,1,0:T(1,128)} %bitcast.5), calls=%async_computation.1 | async-start | bytes 32768 | tf_op jit(solution)/shard_map/all_to_all | solution.py:324
  8.4 1.3 %fusion.1 = s32[1024]{0:T(1024)} fusion(s32[1024]{0:T(1024)} %param.10), kind=kLoop, calls=%fused_computation.5 | loop fusion | flops 8192 | bytes 8192 | tf_op jit(solution)/shard_map/add | solution.py:317
  9.7 14.2 %project_pack.1 = bf16[3584,256]{1,0:T(8,128)(2,1)} custom-call(bf16[8461,1024]{1,0:T(8,128)(2,1)} %bitcast.15, bf16[8461,256]{1,0:T(8,128)(2,1)} %weight_ref.1, s32[1,1024]{1,0:T(1,128)} %bitcast.17), custom_call_target="tpu_custom_call" | custom-call | flops 4436000768 | bytes 23495168 | tf_op jit(solution)/shard_map/project_pack/pallas_call | solution.py:53
  23.9 0.0 all-to-all-done.1
  23.9 5.8 %all-to-all-start = ((bf16[32,112,256]{2,1,0:T(8,128)(2,1)}), bf16[32,112,256]{2,1,0:T(8,128)(2,1)S(1)}, u32[]{:S(2)}, u32[]{:S(2)}) async-start(bf16[32,112,256]{2,1,0:T(8,128)(2,1)} %bitcast.16), calls=%async_computation | async-start | bytes 3670016 | tf_op jit(solution)/shard_map/all_to_all | solution.py:327
  30.4 0.4 broadcast_in_dim.24.live_ref
  30.9 0.0 copy-start
  30.9 4.0 %copy-done = bf16[64,32,2560]{2,1,0:T(8,128)(2,1)S(1)} copy-done((bf16[64,32,2560]{2,1,0:T(8,128)(2,1)S(1)}, bf16[64,32,2560]{2,1,0:T(8,128)(2,1)}, u32[]{:S(2)}) %copy-start) | copy-done | bytes 10485784
  34.8 4.0 %density.1.dens_ref = f32[2048,128]{1,0:T(8,128)S(1)} custom-call(bf16[2048,2560]{1,0:T(8,128)(2,1)S(1)} %bitcast.12, bf16[2560,128]{1,0:T(8,128)(2,1)S(1)} %broadcast_in_dim.24.live_ref), custom_call_target="tpu_custom_call" | custom-call | flops 1342177280 | bytes 10485760 | tf_op jit(solution)/shard_map/density/pallas_call | solution.py:84
  38.8 0.5 broadcast.14
  39.3 0.7 reduce.3
  40.0 0.1 reshape.32.slots_ref
  40.1 31.5 %all-to-all-done = bf16[32,112,256]{2,1,0:T(8,128)(2,1)S(1)} async-done(((bf16[32,112,256]{2,1,0:T(8,128)(2,1)}), bf16[32,112,256]{2,1,0:T(8,128)(2,1)S(1)}, u32[]{:S(2)}, u32[]{:S(2)}) %all-to-all-start) | async-done | bytes 1835040 | tf_op jit(solution)/shard_map/all_to_all | solution.py:327
  71.6 0.0 copy-start.1
  71.6 0.0 copy-start.2
  71.6 9.0 %setconv.1.grid_ref = bf16[2048,256]{1,0:T(8,128)(2,1)S(1)} custom-call(bf16[3584,256]{1,0:T(8,128)(2,1)S(1)} %bitcast.13, s32[1,3584]{1,0:T(1,128)S(1)} %reshape.32.slots_ref, f32[2048,128]{1,0:T(8,128)S(1)} %density.1.dens_ref, bf16[2048,2560]{1,0:T(8,128)(2,1)} %bitcast.11), custom_call_target="tpu_custom_call" | custom-call | flops 5368709120 | bytes 10485760 | tf_op jit(solution)/shard_map/setconv/pallas_call | solution.py:141
  80.6 0.0 copy-done.1
  80.6 0.0 copy-done.2
  80.6 11.1 %encode.1 = bf16[128,256]{1,0:T(8,128)(2,1)S(1)} custom-call(bf16[2048,256]{1,0:T(8,128)(2,1)S(1)} %setconv.1.grid_ref, bf16[3,3,256,256]{3,2,1,0:T(8,128)(2,1)S(1)} %copy-done.1, bf16[3,3,256,256]{3,2,1,0:T(8,128)(2,1)S(1)} %copy-done.2), custom_call_target="tpu_custom_call" | custom-call | tf_op jit(solution)/shard_map/encode/pallas_call | solution.py:289
  91.7 0.6 copy.12
  (1 shorter events, 0.0 us)
Async XLA Ops:
  2.2 21.8 %all-to-all-start.1 = ((s32[32,1,112]{2,1,0:T(1,128)}), s32[32,1,112]{2,1,0:T(1,128)S(1)}, u32[]{:S(2)}, u32[]{:S(2)}) async-start(s32[32,1,112]{2,1,0:T(1,128)} %bitcast.5), calls=%async_computation.1 | async-start | bytes 32768 | tf_op jit(solution)/shard_map/all_to_all | solution.py:324
  23.9 47.6 %all-to-all-start = ((bf16[32,112,256]{2,1,0:T(8,128)(2,1)}), bf16[32,112,256]{2,1,0:T(8,128)(2,1)S(1)}, u32[]{:S(2)}, u32[]{:S(2)}) async-start(bf16[32,112,256]{2,1,0:T(8,128)(2,1)} %bitcast.16), calls=%async_computation | async-start | bytes 3670016 | tf_op jit(solution)/shard_map/all_to_all | solution.py:327
  30.9 4.0 %copy-start = (bf16[64,32,2560]{2,1,0:T(8,128)(2,1)S(1)}, bf16[64,32,2560]{2,1,0:T(8,128)(2,1)}, u32[]{:S(2)}) copy-start(bf16[64,32,2560]{2,1,0:T(8,128)(2,1)} %param.13) | copy-start | bytes 31457284
  71.6 9.0 %copy-start.1 = (bf16[3,3,256,256]{3,2,1,0:T(8,128)(2,1)S(1)}, bf16[3,3,256,256]{3,2,1,0:T(8,128)(2,1)}, u32[]{:S(2)}) copy-start(bf16[3,3,256,256]{3,2,1,0:T(8,128)(2,1)} %k1_ref.1) | copy-start | bytes 3538948
  71.6 9.0 %copy-start.2 = (bf16[3,3,256,256]{3,2,1,0:T(8,128)(2,1)S(1)}, bf16[3,3,256,256]{3,2,1,0:T(8,128)(2,1)}, u32[]{:S(2)}) copy-start(bf16[3,3,256,256]{3,2,1,0:T(8,128)(2,1)} %k2_ref.1) | copy-start | bytes 3538948
